TPU v7x, 512 devices: a whole 4x8x8 slice. The times are simulated.
512 devices in a mesh: img: 16 (over y, core), view: 32 (over z, x).
Axes of the slice: x: 4, y: 8, z: 8, core: 2. Of those that a mesh axis runs over, the one named last changes fastest.
Arguments:
- centers: float32 [3, 65536], P(None, ('img', 'view')), may hold values from -1 to 1
- log_scales: float32 [3, 65536], P(None, ('img', 'view')), may hold values from -3 to 0.9
- quaternions: float32 [4, 65536], P(None, ('img', 'view')), may hold values from 0.5 to 1.5
- logits: float32 [65536], P(('img', 'view')), may hold values from -6 to -3
- harmonics: float32 [48, 65536], P(None, ('img', 'view')), may hold values from -3 to 3
- cameras: float32 [32, 3], replicated, may hold values from -3.140625 to 3.140625
- tile_lists: int32 [32, 16, 4, 256], P('view', 'img'), may hold values from 0 to 2047
- tile_counts: int32 [32, 16, 4], P('view', 'img'), may hold values from 1 to 256, as said below
- tile_ids: int32 [32, 16, 4], P('view', 'img'), may hold values from 0 to 63, as said below
- send_index: int32 [32, 16, 16, 128], P('view', 'img'), may hold values from 0 to 4095
- pixel_grad: float32 [32, 16, 4, 3, 256], P('view', 'img'), may hold values from -6 to 6
Outputs:
- rendered: float32 [32, 16, 4, 3, 256], P('view', 'img')
- grad_centers: float32 [3, 65536], P(None, ('img', 'view'))
- grad_scales: float32 [3, 65536], P(None, ('img', 'view'))
- grad_quaternions: float32 [4, 65536], P(None, ('img', 'view'))
- grad_logits: float32 [65536], P(('img', 'view'))
- grad_harmonics: float32 [48, 65536], P(None, ('img', 'view'))
Inputs may be any that keep to these rules, and one draw needn't show every extreme that they name: `tile_counts`: each owner of each camera has at least one tile whose count is 256. `tile_ids`: for each camera the tile numbers of all owners together are 0 to 63, each once.
All inputs are finite; a program needn't handle non-finite values.
Results may differ from a plain program's by a relative error of at most 0.0003.
Values sent between devices are 32-bit elements; how exact they have to be, the bound alone decides.
A program may use at most 64 MiB of HBM per device.

v0:
```python
import jax
import jax.numpy as jnp
from jax import lax
from jax.sharding import PartitionSpec as P

TW = 8


CAMERA_DISTANCE = 4.0
HARMONIC_ZERO = 0.28209479177387814
HARMONIC_ONE = 0.4886025119029199
HARMONIC_TWO = [
    1.0925484305920792,
    -1.0925484305920792,
    0.31539156525252005,
    -1.0925484305920792,
    0.5462742152960396,
]
HARMONIC_THREE = [
    -0.5900435899266435,
    2.890611442640554,
    -0.4570457994644658,
    0.3731763325901154,
    -0.4570457994644658,
    1.445305721320277,
    -0.5900435899266435,
]


def times_three(left, right):
    return [
        [
            left[r][0] * right[0][c] + left[r][1] * right[1][c] + left[r][2] * right[2][c]
            for c in range(3)
        ]
        for r in range(3)
    ]


def rotation_matrix(angles):
    cos_a, sin_a = (jnp.cos(angles[0]), jnp.sin(angles[0]))
    cos_b, sin_b = (jnp.cos(angles[1]), jnp.sin(angles[1]))
    cos_g, sin_g = (jnp.cos(angles[2]), jnp.sin(angles[2]))
    about_x = [[1.0, 0.0, 0.0], [0.0, cos_b, -sin_b], [0.0, sin_b, cos_b]]
    about_y = [[cos_a, 0.0, sin_a], [0.0, 1.0, 0.0], [-sin_a, 0.0, cos_a]]
    about_z = [[cos_g, -sin_g, 0.0], [sin_g, cos_g, 0.0], [0.0, 0.0, 1.0]]
    return times_three(about_z, times_three(about_y, about_x))


def project(centers, log_scales, quaternions, logits, harmonics, angles, focal_len, half_w, half_h):
    rotation = rotation_matrix(angles)
    camera = [
        rotation[r][0] * centers[0] + rotation[r][1] * centers[1] + rotation[r][2] * centers[2]
        for r in range(3)
    ]
    inv_depth = 1.0 / (camera[2] + CAMERA_DISTANCE)
    screen_u = focal_len * camera[0] * inv_depth + half_w
    screen_v = focal_len * camera[1] * inv_depth + half_h
    unit_q = quaternions / jnp.sqrt(jnp.sum(quaternions * quaternions, axis=0))
    w, x, y, z = (unit_q[0], unit_q[1], unit_q[2], unit_q[3])
    quat_rot = [
        [1.0 - 2.0 * (y * y + z * z), 2.0 * (x * y - w * z), 2.0 * (x * z + w * y)],
        [2.0 * (x * y + w * z), 1.0 - 2.0 * (x * x + z * z), 2.0 * (y * z - w * x)],
        [2.0 * (x * z - w * y), 2.0 * (y * z + w * x), 1.0 - 2.0 * (x * x + y * y)],
    ]
    stretch = jnp.exp(log_scales)
    factor = [[quat_rot[r][c] * stretch[c] for c in range(3)] for r in range(3)]
    jacobian = [
        [focal_len * inv_depth, 0.0, -focal_len * camera[0] * inv_depth * inv_depth],
        [0.0, focal_len * inv_depth, -focal_len * camera[1] * inv_depth * inv_depth],
    ]
    to_screen = [
        [
            jacobian[a][0] * rotation[0][c]
            + jacobian[a][1] * rotation[1][c]
            + jacobian[a][2] * rotation[2][c]
            for c in range(3)
        ]
        for a in range(2)
    ]
    screen_factor = [
        [
            to_screen[a][0] * factor[0][k]
            + to_screen[a][1] * factor[1][k]
            + to_screen[a][2] * factor[2][k]
            for k in range(3)
        ]
        for a in range(2)
    ]
    cov = [
        [
            screen_factor[a][0] * screen_factor[b][0]
            + screen_factor[a][1] * screen_factor[b][1]
            + screen_factor[a][2] * screen_factor[b][2]
            for b in range(2)
        ]
        for a in range(2)
    ]
    cov_a = cov[0][0] + 0.3
    cov_b = cov[0][1]
    cov_c = cov[1][1] + 0.3
    determinant = cov_a * cov_c - cov_b * cov_b
    offsets = [centers[c] + CAMERA_DISTANCE * rotation[2][c] for c in range(3)]
    length = jnp.sqrt(offsets[0] * offsets[0] + offsets[1] * offsets[1] + offsets[2] * offsets[2])
    x, y, z = (offsets[0] / length, offsets[1] / length, offsets[2] / length)
    xx, yy, zz = (x * x, y * y, z * z)
    sh_basis = jnp.stack(
        [
            HARMONIC_ZERO * jnp.ones_like(x),
            -HARMONIC_ONE * y,
            HARMONIC_ONE * z,
            -HARMONIC_ONE * x,
            HARMONIC_TWO[0] * x * y,
            HARMONIC_TWO[1] * y * z,
            HARMONIC_TWO[2] * (2.0 * zz - xx - yy),
            HARMONIC_TWO[3] * x * z,
            HARMONIC_TWO[4] * (xx - yy),
            HARMONIC_THREE[0] * y * (3.0 * xx - yy),
            HARMONIC_THREE[1] * x * y * z,
            HARMONIC_THREE[2] * y * (4.0 * zz - xx - yy),
            HARMONIC_THREE[3] * z * (2.0 * zz - 3.0 * xx - 3.0 * yy),
            HARMONIC_THREE[4] * x * (4.0 * zz - xx - yy),
            HARMONIC_THREE[5] * z * (xx - yy),
            HARMONIC_THREE[6] * x * (xx - 3.0 * yy),
        ]
    )
    colour = jnp.maximum(
        jnp.sum(sh_basis[:, None, :] * harmonics.reshape(16, 3, -1), axis=0) + 0.5, 0.0
    )
    opacity = jax.nn.sigmoid(logits)
    geometry = jnp.stack(
        [screen_u, screen_v, cov_c / determinant, -cov_b / determinant, cov_a / determinant]
    )
    return jnp.concatenate([geometry, colour, opacity[None, :]], axis=0)


def blend(proj_rows, tile_list, counts, tile_num, across):
    entries = jnp.take(proj_rows, tile_list, axis=1)
    length = tile_list.shape[1]
    pixel = jnp.arange(256)
    local_x = (pixel % 16).astype(jnp.float32) + 0.5
    local_y = (pixel // 16).astype(jnp.float32) + 0.5
    pix_x = (16 * (tile_num % across)).astype(jnp.float32)[:, None] + local_x[None, :]
    pix_y = (16 * (tile_num // across)).astype(jnp.float32)[:, None] + local_y[None, :]
    diff_x = pix_x[:, :, None] - entries[0][:, None, :]
    diff_y = pix_y[:, :, None] - entries[1][:, None, :]
    exponent = -0.5 * (
        entries[2][:, None, :] * diff_x * diff_x
        + 2.0 * entries[3][:, None, :] * diff_x * diff_y
        + entries[4][:, None, :] * diff_y * diff_y
    )
    live_mask = (jnp.arange(length)[None, :] < counts[:, None]).astype(jnp.float32)
    alphas = (entries[8] * live_mask)[:, None, :] * jnp.exp(exponent)
    triangle = (jnp.arange(length)[:, None] < jnp.arange(length)[None, :]).astype(jnp.float32)
    log_trans = jnp.einsum(
        "tpk,kj->tpj", jnp.log1p(-alphas), triangle, precision=lax.Precision.HIGHEST
    )
    weights = alphas * jnp.exp(log_trans)
    return jnp.einsum("tpk,ctk->tcp", weights, entries[5:8], precision=lax.Precision.HIGHEST)


def per_device(
    centers,
    log_scales,
    quaternions,
    logits,
    harmonics,
    cameras,
    tile_lists,
    tile_counts,
    tile_ids,
    send_index,
    pixel_grad,
):
    img_count = lax.axis_size("img")
    tile_count = tile_ids.shape[2]
    focal_len = 16.0 * TW
    half_w = 8.0 * TW
    half_h = 8.0 * (img_count * tile_count // TW)
    shard_params = (
        lax.all_gather(centers, "view", axis=1, tiled=True),
        lax.all_gather(log_scales, "view", axis=1, tiled=True),
        lax.all_gather(quaternions, "view", axis=1, tiled=True),
        lax.all_gather(logits, "view", axis=0, tiled=True),
        lax.all_gather(harmonics, "view", axis=1, tiled=True),
    )
    my_angles = lax.dynamic_index_in_dim(cameras, lax.axis_index("view"), 0, keepdims=False)

    def project_shard(*values):
        return project(*values, my_angles, focal_len, half_w, half_h)

    proj_rows, pullback = jax.vjp(project_shard, *shard_params)
    send_slots = send_index[0, 0]
    picked = jnp.take(proj_rows, send_slots, axis=1)
    received = lax.all_to_all(picked, "img", split_axis=1, concat_axis=1, tiled=True).reshape(9, -1)

    def render(rows_in):
        return blend(rows_in, tile_lists[0, 0], tile_counts[0, 0], tile_ids[0, 0], TW)

    rendered, blend_pull = jax.vjp(render, received)
    (row_grad,) = blend_pull(pixel_grad[0, 0])
    returned = lax.all_to_all(
        row_grad.reshape(9, img_count, -1), "img", split_axis=1, concat_axis=1, tiled=True
    )
    shard_grad = (
        jnp.zeros(proj_rows.shape, jnp.float32)
        .at[:, send_slots.reshape(-1)]
        .add(returned.reshape(9, -1))
    )
    grad_one, grad_two, grad_three, grad_four, grad_five = pullback(shard_grad)
    summed = (
        lax.psum_scatter(grad_one, "view", scatter_dimension=1, tiled=True),
        lax.psum_scatter(grad_two, "view", scatter_dimension=1, tiled=True),
        lax.psum_scatter(grad_three, "view", scatter_dimension=1, tiled=True),
        lax.psum_scatter(grad_four, "view", scatter_dimension=0, tiled=True),
        lax.psum_scatter(grad_five, "view", scatter_dimension=1, tiled=True),
    )
    return (rendered[None, None], summed[0], summed[1], summed[2], summed[3], summed[4])


def solution(mesh):
    placed = (
        P(None, ("img", "view")),
        P(None, ("img", "view")),
        P(None, ("img", "view")),
        P(("img", "view")),
        P(None, ("img", "view")),
        P(),
        P("view", "img", None, None),
        P("view", "img", None),
        P("view", "img", None),
        P("view", "img", None, None),
        P("view", "img", None, None, None),
    )
    return jax.shard_map(
        per_device,
        mesh=mesh,
        in_specs=placed,
        out_specs=(
            P("view", "img", None, None, None),
            P(None, ("img", "view")),
            P(None, ("img", "view")),
            P(None, ("img", "view")),
            P(("img", "view")),
            P(None, ("img", "view")),
        ),
        check_vma=False,
    )
```

profile of v0, /device:TPU:1, one launch (start us, length us, event | category | flops | bytes accessed | tf_op | source)
XLA Modules:
  0.0 1254.0 jit_solution(14893711247397935757)
XLA Ops:
  14.9 43.4 %all_gather.15 = f32[3,4096]{1,0:T(4,128)S(1)} all-gather(f32[3,128]{1,0:T(4,128)} %param.11), channel_id=1, replica_groups=mesh['img'=16,'view'=32] {'view'}, dimensions={1}, use_global_device_ids=true | all-gather | bytes 50688 | tf_op jit(solution)/shard_map/all_gather | solution.py:181
  59.1 33.5 %all_gather.18 = f32[48,4096]{1,0:T(8,128)S(1)} all-gather(f32[48,128]{1,0:T(8,128)} %param.15), channel_id=1, replica_groups=mesh['img'=16,'view'=32] {'view'}, dimensions={1}, use_global_device_ids=true | all-gather | bytes 811008 | tf_op jit(solution)/shard_map/all_gather | solution.py:185
  96.0 34.8 %all_gather.16 = f32[4,4096]{1,0:T(4,128)S(1)} all-gather(f32[4,128]{1,0:T(4,128)S(1)} %copy-done.79), channel_id=1, replica_groups=mesh['img'=16,'view'=32] {'view'}, dimensions={1}, use_global_device_ids=true | all-gather | bytes 67584 | tf_op jit(solution)/shard_map/all_gather | solution.py:183
  132.1 35.1 %all_gather.17 = f32[3,4096]{1,0:T(4,128)S(1)} all-gather(f32[3,128]{1,0:T(4,128)S(1)} %copy-done.80), channel_id=1, replica_groups=mesh['img'=16,'view'=32] {'view'}, dimensions={1}, use_global_device_ids=true | all-gather | bytes 50688 | tf_op jit(solution)/shard_map/all_gather | solution.py:182
  177.3 2.8 copy.381
  180.1 27.9 %all-gather = f32[32,1,128]{2,1,0:T(1,128)S(1)} all-gather(f32[1,1,128]{2,1,0:T(1,128)} %bitcast.148), channel_id=1, replica_groups=mesh['img'=16,'view'=32] {'view'}, dimensions={0}, use_global_device_ids=true | all-gather | bytes 16896 | tf_op jit(solution)/shard_map/all_gather | solution.py:184
  211.8 9.2 concatenate.3
  221.0 8.1 gather_fusion
  230.1 61.7 %all-to-all-start = ((f32[9,16,128]{2,0,1:T(8,128)}), f32[9,16,128]{2,0,1:T(8,128)S(1)}, u32[]{:S(2)}, u32[]{:S(2)}) async-start(f32[9,16,128]{2,0,1:T(8,128)} %select_bitcast_fusion), calls=%async_computation | async-start | bytes 262144 | tf_op jit(solution)/shard_map/all_to_all | solution.py:195
  292.0 8.9 all-to-all-done
  301.3 2.8 gather_fusion.1
  308.4 2.8 fusion.15
  311.7 6.3 scatter_custom_fusion
  319.0 3.4 all-to-all-start.1
  323.0 7.8 all-to-all-done.1
  332.3 12.5 %scatter_custom_fusion.1 = f32[9,4096]{0,1:T(8,128)S(1)} fusion(s32[2048]{0:T(1024)} %bitcast.125, f32[2048,9]{1,0:T(8,128)} %copy.393, f32[]{:T(128)} %constant.83.clone.1), kind=kCustom, calls=%fused_computation.46 | custom fusion | flops 18432 | bytes 147968 | tf_op jit(solution)/shard_map/scatter-add | solution.py:208
  344.9 7.3 slice_reduce_fusion
  354.2 3.0 copy.417
  357.1 2.8 copy.418
  394.9 112.4 %all-reduce.32 = f32[4096]{0:T(1024)S(1)} all-reduce(f32[4096]{0:T(1024)S(1)} %fusion.41), channel_id=5, replica_groups=mesh['img'=16,'view'=32] {'view'}, use_global_device_ids=true, to_apply=%region_15.16.clone | all-reduce | flops 4096 | bytes 32768
  507.9 78.8 %reduce-scatter.15.cloned.1.call-done = f32[128,3]{1,0:T(8,128)} async-done(((f32[4096,3]{1,0:T(8,128)}), f32[128,3]{1,0:T(8,128)}) %reduce-scatter.15.cloned.1.call-update) | async-done | bytes 1552
  588.2 223.5 %reduce-scatter.13.cloned.1.call-done = f32[128,3]{1,0:T(8,128)} async-done(((f32[4096,3]{1,0:T(8,128)}), f32[128,3]{1,0:T(8,128)}) %reduce-scatter.13.cloned.1.call-update) | async-done | bytes 1552
  813.2 223.0 %reduce-scatter.17.cloned.1.call-done = f32[128,4]{1,0:T(8,128)} async-done(((f32[4096,4]{1,0:T(8,128)}), f32[128,4]{1,0:T(8,128)}) %reduce-scatter.17.cloned.1.call-update) | async-done | bytes 2064
  1037.8 209.7 %reduce-scatter.11.cloned.1.call-done = f32[48,128]{1,0:T(8,128)} async-done(((f32[48,4096]{1,0:T(8,128)}), f32[48,128]{1,0:T(8,128)}) %reduce-scatter.11.cloned.1.call-update) | async-done | bytes 24592 | tf_op jit(solution)/shard_map/reduce_scatter | solution.py:216
  (285 shorter events, 72.1 us)
Async XLA Ops:
  7.2 297.3 %copy-start = (f32[1,1,4,3,256]{4,2,3,1,0:T(4,128)S(1)}, f32[1,1,4,3,256]{4,2,3,1,0:T(4,128)}, u32[]{:S(2)}) copy-start(f32[1,1,4,3,256]{4,2,3,1,0:T(4,128)} %param.21) | copy-start | bytes 36868
  94.3 36.5 %copy-start.1 = (f32[3,4096]{0,1:T(8,128)}, f32[3,4096]{0,1:T(8,128)S(1)}, u32[]{:S(2)}) copy-start(f32[3,4096]{0,1:T(8,128)S(1)} %copy.375) | copy-start | bytes 147460
  94.3 37.8 %copy-start.80 = (f32[3,128]{1,0:T(4,128)S(1)}, f32[3,128]{1,0:T(4,128)}, u32[]{:S(2)}) copy-start(f32[3,128]{1,0:T(4,128)} %param.12) | copy-start | bytes 4612
  94.4 72.9 %copy-start.9 = (f32[3,4096]{1,0:T(4,128)S(1)}, f32[3,4096]{1,0:T(4,128)}, u32[]{:S(2)}) copy-start(f32[3,4096]{1,0:T(4,128)} %copy-done.8) | copy-start | bytes 147460
  130.9 36.4 %copy-start.32 = (f32[4096]{0:T(1024)}, f32[4096]{0:T(1024)S(1)}, u32[]{:S(2)}) copy-start(f32[4096]{0:T(1024)S(1)} %multiply_reduce_fusion.4) | copy-start | bytes 49156
  167.3 5.8 copy-start.12
  167.3 5.8 copy-start.11
  177.2 34.5 %copy-start.6 = (f32[3,4096]{0,1:T(8,128)S(1)}, f32[3,4096]{0,1:T(8,128)}, u32[]{:S(2)}) copy-start(f32[3,4096]{0,1:T(8,128)} %add_maximum_fusion) | copy-start | bytes 147460
  221.0 70.8 %copy-start.64 = (s32[1,1,4,256]{3,2,1,0:T(4,128)S(1)}, s32[1,1,4,256]{3,2,1,0:T(4,128)}, u32[]{:S(2)}) copy-start(s32[1,1,4,256]{3,2,1,0:T(4,128)} %param.17) | copy-start | bytes 12292
  221.0 70.8 %copy-start.82 = (s32[1,1,4]{2,1,0:T(1,128)S(1)}, s32[1,1,4]{2,1,0:T(1,128)}, u32[]{:S(2)}) copy-start(s32[1,1,4]{2,1,0:T(1,128)} %param.19) | copy-start | bytes 52
  229.4 76.1 %copy-start.81 = (s32[1,1,4]{2,1,0:T(1,128)S(1)}, s32[1,1,4]{2,1,0:T(1,128)}, u32[]{:S(2)}) copy-start(s32[1,1,4]{2,1,0:T(1,128)} %param.18) | copy-start | bytes 52
  230.1 70.9 %all-to-all-start = ((f32[9,16,128]{2,0,1:T(8,128)}), f32[9,16,128]{2,0,1:T(8,128)S(1)}, u32[]{:S(2)}, u32[]{:S(2)}) async-start(f32[9,16,128]{2,0,1:T(8,128)} %select_bitcast_fusion), calls=%async_computation | async-start | bytes 262144 | tf_op jit(solution)/shard_map/all_to_all | solution.py:195
  292.0 16.3 %copy-start.65 = (f32[4,256]{1,0:T(4,128)}, f32[4,256]{1,0:T(4,128)S(1)}, u32[]{:S(2)}) copy-start(f32[4,256]{1,0:T(4,128)S(1)} %broadcast_add_fusion.4) | copy-start | bytes 12292
  311.2 11.2 copy-start.47
  319.0 11.9 all-to-all-start.1
  322.4 264.3 %reduce-scatter.15.cloned.1.call-start = ((), (), s32[]{:S(2)}) async-start(), calls=%async_computation.8 | async-start | bytes 2162688
  344.9 7.3 copy-start.2
  354.2 5.8 copy-start.5
  365.2 8.0 copy-start.41
  365.2 8.0 copy-start.43
  376.2 435.6 %reduce-scatter.13.cloned.1.call-start = ((), (), s32[]{:S(2)}) async-start(), calls=%async_computation.7 | async-start | bytes 2162688
  377.5 5.8 copy-start.3
  387.2 649.1 %reduce-scatter.17.cloned.1.call-start = ((), (), s32[]{:S(2)}) async-start(), calls=%async_computation.9 | async-start | bytes 2162688
  389.4 858.1 %reduce-scatter.11.cloned.1.call-start = ((), (), s32[]{:S(2)}) async-start(), calls=%async_computation.6 | async-start | bytes 811008 | tf_op jit(solution)/shard_map/reduce_scatter | solution.py:216
  (67 other events, 185.8 us)
Sparse Core Ops, SparseCore 0:
  376.3 210.3 reduce-scatter.14
  591.8 219.9 reduce-scatter.12
  816.2 220.0 reduce-scatter.16
  1041.7 205.7 reduce-scatter.10
where the time goes:
time: 1260 us; the launch traced here: 1250 us
  waiting for transfers between devices  752 us (60%)
  blocking collectives  287 us (23%)
  local copies, waits for them, and re-layouts  74.5 us (6%)
  starting transfers between devices  65.3 us (5%)
  other arithmetic  47.1 us (4%)
  between operations  20.2 us (2%)
    unnamed x7, waiting for transfers between devices  525 us
    reduce_scatter x1, waiting for transfers between devices, per_device(): lax.psum_scatter(grad_five, 'view', scatter_dimension=1, tiled=True)  210 us
    unnamed x1, blocking collectives  112 us
    all_to_all x1, starting transfers between devices, per_device(): lax.all_to_all(picked, 'img', split_axis=1, concat_axis=1, tiled=True)  61.7 us
    all_gather x1, blocking collectives, per_device(): lax.all_gather(centers, 'view', axis=1, tiled=True)  43.4 us
    all_gather x1, blocking collectives, per_device(): lax.all_gather(log_scales, 'view', axis=1, tiled=True)  35.1 us
    all_gather x1, blocking collectives, per_device(): lax.all_gather(quaternions, 'view', axis=1, tiled=True)  34.8 us
    all_gather x1, blocking collectives, per_device(): lax.all_gather(harmonics, 'view', axis=1, tiled=True)  33.5 us
  transfers between devices with their start and end apart: 6, of which 6 were waited for; matrix products, arithmetic and copies ran while one was open for 2% of the time, Pallas kernels for 0%

commit v1 on v0

v1 whole, which is shorter than its diff:
```python
import functools

import jax
import jax.numpy as jnp
from jax import lax
from jax.experimental import pallas as pl
from jax.experimental.pallas import tpu as pltpu
from jax.sharding import PartitionSpec as P

TW = 8
ROWS = 9
LANES = 128
PIX = 256
FINE_ROWS = (2, 3, 4)
LOG2E = 1.4426950408889634
CAMERA_DISTANCE = 4.0
C0 = 0.28209479177387814
C1 = 0.4886025119029199
C20, C21, C22, C23, C24 = (
    1.0925484305920792,
    -1.0925484305920792,
    0.31539156525252005,
    -1.0925484305920792,
    0.5462742152960396,
)
C30, C31, C32, C33, C34, C35, C36 = (
    -0.5900435899266435,
    2.890611442640554,
    -0.4570457994644658,
    0.3731763325901154,
    -0.4570457994644658,
    1.445305721320277,
    -0.5900435899266435,
)
F32 = jnp.float32
BF16 = jnp.bfloat16


def split_two(value):
    high = value.astype(BF16)
    low = (value - high.astype(F32)).astype(BF16)
    return high, low


def dot(left, right):
    return lax.dot_general(left, right, (((1,), (0,)), ((), ())), preferred_element_type=F32)


def dot_nt(left, right):
    return lax.dot_general(left, right, (((1,), (1,)), ((), ())), preferred_element_type=F32)


def rotations(cameras, count):
    cosines, sines = jnp.cos(cameras), jnp.sin(cameras)

    def column(values, k):
        return jnp.broadcast_to(values[:, k : k + 1], (count, LANES))

    ca, cb, cg = (column(cosines, k) for k in range(3))
    sa, sb, sg = (column(sines, k) for k in range(3))
    return [
        [cg * ca, cg * sa * sb - sg * cb, cg * sa * cb + sg * sb],
        [sg * ca, sg * sa * sb + cg * cb, sg * sa * cb - cg * sb],
        [-sa, ca * sb, ca * cb],
    ]


def shape_factor(quats, scales):
    inv = lax.rsqrt(sum(q * q for q in quats))
    w, x, y, z = (q * inv for q in quats)
    rot = [
        [1.0 - 2.0 * (y * y + z * z), 2.0 * (x * y - w * z), 2.0 * (x * z + w * y)],
        [2.0 * (x * y + w * z), 1.0 - 2.0 * (x * x + z * z), 2.0 * (y * z - w * x)],
        [2.0 * (x * z - w * y), 2.0 * (y * z + w * x), 1.0 - 2.0 * (x * x + y * y)],
    ]
    stretch = [jnp.exp(s) for s in scales]
    factor = [[rot[r][k] * stretch[k] for k in range(3)] for r in range(3)]
    return (w, x, y, z), inv, stretch, factor


def basis_of(x, y, z):
    xx, yy, zz = x * x, y * y, z * z
    return [
        None,
        -C1 * y,
        C1 * z,
        -C1 * x,
        C20 * x * y,
        C21 * y * z,
        C22 * (2.0 * zz - xx - yy),
        C23 * x * z,
        C24 * (xx - yy),
        C30 * y * (3.0 * xx - yy),
        C31 * x * y * z,
        C32 * y * (4.0 * zz - xx - yy),
        C33 * z * (2.0 * zz - 3.0 * xx - 3.0 * yy),
        C34 * x * (4.0 * zz - xx - yy),
        C35 * z * (xx - yy),
        C36 * x * (xx - 3.0 * yy),
    ]


def project(rot, centers, factor, harm_ref, focal, half_w, half_h):
    pts = [rot[r][0] * centers[0] + rot[r][1] * centers[1] + rot[r][2] * centers[2] for r in range(3)]
    iz = 1.0 / (pts[2] + CAMERA_DISTANCE)
    fiz = focal * iz
    tx, ty = pts[0] * iz, pts[1] * iz
    t0 = [fiz * (rot[0][c] - tx * rot[2][c]) for c in range(3)]
    t1 = [fiz * (rot[1][c] - ty * rot[2][c]) for c in range(3)]
    s0 = [t0[0] * factor[0][k] + t0[1] * factor[1][k] + t0[2] * factor[2][k] for k in range(3)]
    s1 = [t1[0] * factor[0][k] + t1[1] * factor[1][k] + t1[2] * factor[2][k] for k in range(3)]
    cov_a = s0[0] * s0[0] + s0[1] * s0[1] + s0[2] * s0[2] + 0.3
    cov_b = s0[0] * s1[0] + s0[1] * s1[1] + s0[2] * s1[2]
    cov_c = s1[0] * s1[0] + s1[1] * s1[1] + s1[2] * s1[2] + 0.3
    inv_det = 1.0 / (cov_a * cov_c - cov_b * cov_b)
    conic = (cov_c * inv_det, -cov_b * inv_det, cov_a * inv_det)
    offs = [centers[c] + CAMERA_DISTANCE * rot[2][c] for c in range(3)]
    inv_len = lax.rsqrt(offs[0] * offs[0] + offs[1] * offs[1] + offs[2] * offs[2])
    x, y, z = (o * inv_len for o in offs)
    basis = basis_of(x, y, z)
    shade = []
    for ch in range(3):
        total = 0.5 + C0 * harm_ref[ch : ch + 1, :]
        for l in range(1, 16):
            total = total + basis[l] * harm_ref[3 * l + ch : 3 * l + ch + 1, :]
        shade.append(total)
    colour = [jnp.maximum(s, 0.0) for s in shade]
    values = [focal * tx + half_w, focal * ty + half_h, *conic, *colour]
    saved = (iz, fiz, tx, ty, t0, t1, s0, s1, conic, inv_det, inv_len, (x, y, z), basis, shade)
    return values, saved


def over_cameras(value):
    return jnp.sum(value, axis=0, keepdims=True)


def project_back(rot, factor, harm_ref, focal, saved, grads, grad_harm_ref):
    iz, fiz, tx, ty, t0, t1, s0, s1, conic, inv_det, inv_len, (x, y, z), basis, shade = saved
    du, dv, dca, dcb, dcc = grads[:5]
    dcol = []
    for ch in range(3):
        g = grads[5 + ch]
        dcol.append(jnp.where(shade[ch] > 0.0, g, jnp.where(shade[ch] == 0.0, 0.5 * g, 0.0)))
    e = [None]
    for ch in range(3):
        grad_harm_ref[ch : ch + 1, :] = C0 * over_cameras(dcol[ch])
    for l in range(1, 16):
        e.append(sum(harm_ref[3 * l + ch : 3 * l + ch + 1, :] * dcol[ch] for ch in range(3)))
        for ch in range(3):
            grad_harm_ref[3 * l + ch : 3 * l + ch + 1, :] = over_cameras(basis[l] * dcol[ch])
    xx, yy, zz, xy, yz, xz = x * x, y * y, z * z, x * y, y * z, x * z
    dx = (
        -C1 * e[3]
        + C20 * y * e[4]
        + x * (2.0 * C24 * e[8] - 2.0 * C22 * e[6])
        + C23 * z * e[7]
        + xy * (6.0 * C30 * e[9] - 2.0 * C32 * e[11])
        + C31 * yz * e[10]
        + xz * (2.0 * C35 * e[14] - 6.0 * C33 * e[12])
        + C34 * (4.0 * zz - 3.0 * xx - yy) * e[13]
        + 3.0 * C36 * (xx - yy) * e[15]
    )
    dy = (
        -C1 * e[1]
        + C20 * x * e[4]
        + C21 * z * e[5]
        - y * (2.0 * C22 * e[6] + 2.0 * C24 * e[8])
        + 3.0 * C30 * (xx - yy) * e[9]
        + C31 * xz * e[10]
        + C32 * (4.0 * zz - xx - 3.0 * yy) * e[11]
        - yz * (6.0 * C33 * e[12] + 2.0 * C35 * e[14])
        - xy * (2.0 * C34 * e[13] + 6.0 * C36 * e[15])
    )
    dz = (
        C1 * e[2]
        + C21 * y * e[5]
        + 4.0 * C22 * z * e[6]
        + C23 * x * e[7]
        + C31 * xy * e[10]
        + 8.0 * C32 * yz * e[11]
        + C33 * (6.0 * zz - 3.0 * xx - 3.0 * yy) * e[12]
        + 8.0 * C34 * xz * e[13]
        + C35 * (xx - yy) * e[14]
    )
    along = x * dx + y * dy + z * dz
    doff = [inv_len * (dx - x * along), inv_len * (dy - y * along), inv_len * (dz - z * along)]
    ca, cb, cc = conic
    s = dca * ca + dcb * cb + dcc * cc
    da = inv_det * dcc - s * ca
    dc = inv_det * dca - s * cc
    db = -(inv_det * dcb) - 2.0 * s * cb
    da2, dc2 = da + da, dc + dc
    ds0 = [da2 * s0[k] + db * s1[k] for k in range(3)]
    ds1 = [dc2 * s1[k] + db * s0[k] for k in range(3)]
    dt0 = [sum(ds0[k] * factor[c][k] for k in range(3)) for c in range(3)]
    dt1 = [sum(ds1[k] * factor[c][k] for k in range(3)) for c in range(3)]
    dfactor = [[over_cameras(t0[c] * ds0[k] + t1[c] * ds1[k]) for k in range(3)] for c in range(3)]
    n0 = sum(dt0[c] * rot[2][c] for c in range(3))
    n1 = sum(dt1[c] * rot[2][c] for c in range(3))
    m0 = sum(dt0[c] * rot[0][c] for c in range(3))
    m1 = sum(dt1[c] * rot[1][c] for c in range(3))
    dfiz = (m0 - tx * n0) + (m1 - ty * n1)
    dtx = focal * du - fiz * n0
    dty = focal * dv - fiz * n1
    dp = [dtx * iz, dty * iz, -iz * (fiz * dfiz + dtx * tx + dty * ty)]
    dcenters = [
        over_cameras(sum(rot[r][c] * dp[r] for r in range(3)) + doff[c]) for c in range(3)
    ]
    return dcenters, dfactor


def shape_back(unit, inv, stretch, factor, dfactor):
    w, x, y, z = unit
    dscale = [sum(factor[r][k] * dfactor[r][k] for r in range(3)) for k in range(3)]
    d = [[dfactor[r][k] * stretch[k] for k in range(3)] for r in range(3)]
    dw = 2.0 * (z * (d[1][0] - d[0][1]) + y * (d[0][2] - d[2][0]) + x * (d[2][1] - d[1][2]))
    dx = 2.0 * (
        y * (d[0][1] + d[1][0]) + z * (d[0][2] + d[2][0]) + w * (d[2][1] - d[1][2])
    ) - 4.0 * x * (d[1][1] + d[2][2])
    dy = 2.0 * (
        x * (d[0][1] + d[1][0]) + z * (d[1][2] + d[2][1]) + w * (d[0][2] - d[2][0])
    ) - 4.0 * y * (d[0][0] + d[2][2])
    dz = 2.0 * (
        x * (d[0][2] + d[2][0]) + y * (d[1][2] + d[2][1]) + w * (d[1][0] - d[0][1])
    ) - 4.0 * z * (d[0][0] + d[1][1])
    along = w * dw + x * dx + y * dy + z * dz
    dquat = [inv * (g - q * along) for g, q in zip((dw, dx, dy, dz), unit)]
    return dscale, dquat


def lane_pick(table, lanes):
    return jnp.take_along_axis(table, lanes, axis=1, mode="promise_in_bounds")


def triangle(later):
    row = lax.broadcasted_iota(jnp.int32, (PIX, PIX), 0)
    col = lax.broadcasted_iota(jnp.int32, (PIX, PIX), 1)
    return jnp.where(row > col if later else row < col, 1.0, 0.0).astype(BF16)


def render_tile(geometry, opacity, count, tile, grad, grad_t, before, after):
    entry = lax.broadcasted_iota(jnp.int32, (1, PIX), 1)
    live = jnp.where(entry < count, opacity, 0.0)
    left = (16 * lax.rem(tile, TW) + 8).astype(F32)
    top = (16 * lax.div(tile, TW) + 8).astype(F32)
    u, v = geometry[0:1] - left, geometry[1:2] - top
    ca, cb, cc = geometry[2:3], geometry[3:4], geometry[4:5]
    colour = geometry[5:8]
    local = lax.broadcasted_iota(jnp.int32, (16, PIX), 0).astype(F32) - 7.5
    dx, dy = local - u, local - v
    part_a = (-0.5 * LOG2E * ca) * dx * dx
    part_b = (-LOG2E * cb) * dx
    part_c = (-0.5 * LOG2E * cc) * dy * dy
    c_hi, c_lo = split_two(colour)
    mix = jnp.concatenate([c_hi, c_lo, c_hi], axis=0)
    reach = dot(grad_t, mix)
    moments = [None, None, None]
    w_hi_all, w_lo_all = [], []
    for at in range(0, 16, 4):
        alphas, logs = [], []
        for line in range(at, at + 4):
            power = part_a + part_b * dy[line : line + 1] + part_c[line : line + 1]
            alphas.append(live * jnp.exp2(power))
        alpha = jnp.concatenate(alphas, axis=0)
        left_over = 1.0 - alpha
        log_left = jnp.log2(left_over)
        log_hi, log_lo = split_two(log_left)
        weight = alpha * jnp.exp2(dot(log_hi, before) + dot(log_lo, before))
        gain = weight * reach[16 * at : 16 * at + 64]
        g_hi, g_lo = split_two(gain)
        behind = dot(g_hi, after) + dot(g_lo, after)
        back = gain - behind * (alpha / left_over)
        w_hi, w_lo = split_two(weight)
        w_hi_all.append(w_hi)
        w_lo_all.append(w_lo)
        for k in range(4):
            piece = back[16 * k : 16 * k + 16]
            level = at + k - 7.5
            terms = (piece, level * piece, (level * level) * piece)
            for m in range(3):
                moments[m] = terms[m] if moments[m] is None else moments[m] + terms[m]
    w_hi = jnp.concatenate(w_hi_all, axis=0)
    w_lo = jnp.concatenate(w_lo_all, axis=0)
    both = jnp.concatenate([c_hi, c_lo], axis=0)
    first = dot_nt(both, w_hi)
    picture = first[0:3] + first[3:6] + dot_nt(c_hi, w_lo)
    pg_hi, pg_lo = split_two(grad)
    both = jnp.concatenate([pg_hi, pg_lo], axis=0)
    first = dot(both, w_hi)
    dcolour = first[0:3] + first[3:6] + dot(pg_hi, w_lo)

    def total(value):
        return jnp.sum(value, axis=0, keepdims=True)

    m0, my, myy = (total(m) for m in moments)
    mx, mxy = total(local * moments[0]), total(local * moments[1])
    mxx = total(local * local * moments[0])
    qx, qy = mx - u * m0, my - v * m0
    qxx = mxx - u * (mx + qx)
    qyy = myy - v * (my + qy)
    qxy = mxy - u * my - v * qx
    grads = [
        ca * qx + cb * qy,
        cb * qx + cc * qy,
        -0.5 * qxx,
        -qxy,
        -0.5 * qyy,
        dcolour[0:1],
        dcolour[1:2],
        dcolour[2:3],
        m0 / opacity,
    ]
    return picture, grads


def exchange(axis, me, size, source, landing, send_sem, recv_sem):
    def copy(peer, slot):
        return pltpu.make_async_remote_copy(
            src_ref=source(peer),
            dst_ref=landing.at[slot],
            send_sem=send_sem.at[peer],
            recv_sem=recv_sem.at[slot],
            device_id={axis: peer},
            device_id_type=pl.DeviceIdType.MESH,
        )

    def start(step, carry):
        copy(lax.rem(me + step, size), me).start()
        return carry

    def sent(step, carry):
        copy(lax.rem(me + step, size), me).wait_send()
        return carry

    lax.fori_loop(1, size, start, 0)

    def arrived(peer):
        copy(peer, peer).wait_recv()

    return arrived, lambda: lax.fori_loop(1, size, sent, 0)


def greet(axis, me, size, barrier):
    def signal(step, carry):
        pl.semaphore_signal(
            barrier,
            inc=1,
            device_id={axis: lax.rem(me + step, size)},
            device_id_type=pl.DeviceIdType.MESH,
        )
        return carry

    lax.fori_loop(1, size, signal, 0)


def picker(index, size):
    blocks = index.shape[0]
    high, low = lax.shift_right_logical(index, 7), lax.bitwise_and(index, 127)
    highs = [jnp.broadcast_to(high[b : b + 1], (8, LANES)) for b in range(blocks)]
    lows = [jnp.broadcast_to(low[b : b + 1], (8, LANES)) for b in range(blocks)]

    def add(number, table, picks):
        geometry, opacity = picks
        front = table[0:8]
        last = jnp.broadcast_to(table[8:9], (8, LANES))
        geometry = tuple(
            jnp.where(highs[b] == number, lane_pick(front, lows[b]), geometry[b])
            for b in range(blocks)
        )
        opacity = tuple(
            jnp.where(
                high[8 * g : 8 * g + 8] == number, lane_pick(last, low[8 * g : 8 * g + 8]), opacity[g]
            )
            for g in range(blocks // 8)
        )
        return geometry, opacity

    zero = jnp.zeros((8, LANES), F32)
    return add, ((zero,) * blocks, (zero,) * (blocks // 8))


def scatter_sides(index, groups):
    count = index.shape[1]
    high, low = lax.shift_right_logical(index, 8), lax.bitwise_and(index, 255)
    mask = lax.broadcasted_iota(jnp.int32, (groups, count), 0) == high
    hot = lax.broadcasted_iota(jnp.int32, (256, count), 0) == low
    return mask, jnp.where(hot, 1.0, 0.0).astype(BF16)


def scatter(rows, mask, hot):
    groups = mask.shape[0]
    sides, owners = [], []
    for r, row in enumerate(rows):
        for _ in range(3 if r in FINE_ROWS else 2):
            high = row.astype(BF16).astype(F32)
            sides.append(jnp.where(mask, high, 0.0))
            owners.append(r)
            row = row - high
    if len(sides) * groups % 16:
        sides.append(jnp.zeros_like(sides[0]))
    out = dot_nt(jnp.concatenate(sides, axis=0).astype(BF16), hot)
    return [
        sum(out[groups * k : groups * (k + 1)] for k, owner in enumerate(owners) if owner == r)
        for r in range(len(rows))
    ]


def train_kernel(
    n_img,
    n_view,
    sizes,
    cameras_ref,
    centers_ref,
    scales_ref,
    quats_ref,
    logits_ref,
    harm_ref,
    lists_ref,
    counts_ref,
    ids_ref,
    slots_ref,
    grad_ref,
    picture_ref,
    out_centers_ref,
    out_scales_ref,
    out_quats_ref,
    out_logits_ref,
    out_harm_ref,
    send_one,
    recv_one,
    send_two,
    recv_two,
    send_three,
    recv_three,
    send_four,
    recv_four,
    view_sems,
    img_sems,
):
    focal, half_w, half_h = sizes
    img, view = lax.axis_index("img"), lax.axis_index("view")
    barrier = pltpu.get_barrier_semaphore()
    greet("view", view, n_view, barrier)
    greet("img", img, n_img, barrier)

    rot = rotations(cameras_ref[...], n_view)
    centers = [centers_ref[c : c + 1, :] for c in range(3)]
    unit, inv_norm, stretch, factor = shape_factor(
        [quats_ref[k : k + 1, :] for k in range(4)], [scales_ref[k : k + 1, :] for k in range(3)]
    )
    opacity = 1.0 / (1.0 + jnp.exp(-logits_ref[...]))
    values, saved = project(rot, centers, factor, harm_ref, focal, half_w, half_h)
    for r, value in enumerate(values):
        send_one[:, r, :] = value
    send_one[:, 8, :] = jnp.broadcast_to(opacity, (n_view, LANES))

    pl.semaphore_wait(barrier, n_view + n_img - 2)
    arrived, sent_one = exchange(
        "view", view, n_view, lambda p: send_one.at[p], recv_one, view_sems.at[0], view_sems.at[1]
    )

    add, picks = picker(slots_ref[...], n_view)
    picks = add(view, send_one[view], picks)

    def take_view(step, picks):
        peer = lax.rem(view + step, n_view)
        arrived(peer)
        return add(peer, recv_one[peer], picks)

    geometry, last = lax.fori_loop(1, n_view, take_view, picks)
    for d in range(n_img):
        send_two[d, 0:8, :] = geometry[d]
        send_two[d, 8:9, :] = last[d // 8][d % 8 : d % 8 + 1]

    arrived, sent_two = exchange(
        "img", img, n_img, lambda p: send_two.at[p], recv_two, img_sems.at[0], img_sems.at[1]
    )

    tiles = lists_ref.shape[0]
    lists = lists_ref[...]
    blocks = jnp.concatenate(
        [lists[t : t + 1, LANES * h : LANES * h + LANES] for t in range(tiles) for h in range(2)], axis=0
    )
    entry_index = jnp.concatenate([lists[t : t + 1] for t in range(tiles)], axis=1)
    entry_mask, entry_hot = scatter_sides(entry_index, n_img // 2)
    before, after = triangle(False), triangle(True)
    add, picks = picker(blocks, n_img)
    picks = add(img, send_two[img], picks)

    def take_img(step, picks):
        peer = lax.rem(img + step, n_img)
        arrived(peer)
        return add(peer, recv_two[peer], picks)

    geometry, last = lax.fori_loop(1, n_img, take_img, picks)
    row_grads = [[] for _ in range(ROWS)]
    for t in range(tiles):
        entries = jnp.concatenate([geometry[2 * t], geometry[2 * t + 1]], axis=1)
        solid = jnp.concatenate([last[0][2 * t : 2 * t + 1], last[0][2 * t + 1 : 2 * t + 2]], axis=1)
        grad = grad_ref[t]
        high = grad.astype(BF16).astype(F32)
        grad_t = jnp.concatenate([high, high, grad - high], axis=0).T.astype(BF16)
        picture, grads = render_tile(
            entries, solid, counts_ref[t], ids_ref[t], grad, grad_t, before, after
        )
        picture_ref[t] = picture
        for r in range(ROWS):
            row_grads[r].append(grads[r])

    rows = [jnp.concatenate(parts, axis=1) for parts in row_grads]
    for r, total in enumerate(scatter(rows, entry_mask, entry_hot)):
        for h in range(2):
            send_three[:, h, r, :] = total[:, LANES * h : LANES * h + LANES]
    arrived, sent_three = exchange(
        "img",
        img,
        n_img,
        lambda p: send_three.at[lax.div(p, 2), lax.rem(p, 2)],
        recv_three,
        img_sems.at[2],
        img_sems.at[3],
    )
    recv_three[img] = send_three[lax.div(img, 2), lax.rem(img, 2)]
    slot_index = jnp.concatenate([slots_ref[d : d + 1, :] for d in range(n_img)], axis=1)
    slot_mask, slot_hot = scatter_sides(slot_index, n_view // 2)

    def take_back(step, carry):
        arrived(lax.rem(img + step, n_img))
        return carry

    lax.fori_loop(1, n_img, take_back, 0)

    rows = [
        jnp.concatenate([recv_three[d, r : r + 1, :] for d in range(n_img)], axis=1) for r in range(ROWS)
    ]
    for r, total in enumerate(scatter(rows, slot_mask, slot_hot)):
        for h in range(2):
            send_four[:, h, r, :] = total[:, LANES * h : LANES * h + LANES]
    arrived, sent_four = exchange(
        "view",
        view,
        n_view,
        lambda p: send_four.at[lax.div(p, 2), lax.rem(p, 2)],
        recv_four,
        view_sems.at[2],
        view_sems.at[3],
    )
    recv_four[view] = send_four[lax.div(view, 2), lax.rem(view, 2)]

    def take_home(step, carry):
        arrived(lax.rem(view + step, n_view))
        return carry

    lax.fori_loop(1, n_view, take_home, 0)

    grads = [recv_four[:, r, :] for r in range(ROWS)]
    dcenters, dfactor = project_back(rot, factor, harm_ref, focal, saved, grads, out_harm_ref)
    dscale, dquat = shape_back(unit, inv_norm, stretch, factor, dfactor)
    for c in range(3):
        out_centers_ref[c : c + 1, :] = dcenters[c]
        out_scales_ref[c : c + 1, :] = dscale[c]
    for k in range(4):
        out_quats_ref[k : k + 1, :] = dquat[k]
    out_logits_ref[...] = over_cameras(grads[8]) * opacity * (1.0 - opacity)
    sent_one()
    sent_two()
    sent_three()
    sent_four()


def per_device(
    centers,
    log_scales,
    quaternions,
    logits,
    harmonics,
    cameras,
    tile_lists,
    tile_counts,
    tile_ids,
    send_index,
    pixel_grad,
):
    n_img, n_view = lax.axis_size("img"), lax.axis_size("view")
    tiles = tile_ids.shape[2]
    sizes = (16.0 * TW, 8.0 * TW, 8.0 * (n_img * tiles // TW))
    vmem, smem = pl.BlockSpec(memory_space=pltpu.VMEM), pl.BlockSpec(memory_space=pltpu.SMEM)
    per_view, per_img = (n_view, ROWS, LANES), (n_img, ROWS, LANES)
    out = pl.pallas_call(
        functools.partial(train_kernel, n_img, n_view, sizes),
        out_shape=(
            jax.ShapeDtypeStruct((tiles, 3, PIX), F32),
            jax.ShapeDtypeStruct((3, LANES), F32),
            jax.ShapeDtypeStruct((3, LANES), F32),
            jax.ShapeDtypeStruct((4, LANES), F32),
            jax.ShapeDtypeStruct((1, LANES), F32),
            jax.ShapeDtypeStruct((48, LANES), F32),
        ),
        in_specs=[vmem] * 7 + [smem] * 2 + [vmem] * 2,
        out_specs=(vmem,) * 6,
        scratch_shapes=[
            pltpu.VMEM(per_view, F32),
            pltpu.VMEM(per_view, F32),
            pltpu.VMEM(per_img, F32),
            pltpu.VMEM(per_img, F32),
            pltpu.VMEM((n_img // 2, 2, ROWS, LANES), F32),
            pltpu.VMEM(per_img, F32),
            pltpu.VMEM((n_view // 2, 2, ROWS, LANES), F32),
            pltpu.VMEM(per_view, F32),
            pltpu.SemaphoreType.DMA((4, n_view)),
            pltpu.SemaphoreType.DMA((4, n_img)),
        ],
        compiler_params=pltpu.CompilerParams(
            collective_id=0, has_side_effects=True, vmem_limit_bytes=40 * 1024 * 1024
        ),
    )(
        cameras,
        centers,
        log_scales,
        quaternions,
        logits.reshape(1, -1),
        harmonics,
        tile_lists[0, 0],
        tile_counts[0, 0],
        tile_ids[0, 0],
        send_index[0, 0],
        pixel_grad[0, 0],
    )
    return (out[0][None, None], out[1], out[2], out[3], out[4].reshape(-1), out[5])


def solution(mesh):
    split = P(None, ("img", "view"))
    placed = (
        split,
        split,
        split,
        P(("img", "view")),
        split,
        P(),
        P("view", "img", None, None),
        P("view", "img", None),
        P("view", "img", None),
        P("view", "img", None, None),
        P("view", "img", None, None, None),
    )
    return jax.shard_map(
        per_device,
        mesh=mesh,
        in_specs=placed,
        out_specs=(P("view", "img", None, None, None), split, split, split, P(("img", "view")), split),
        check_vma=False,
    )
```

time: 1260 us -> 55.3 us (0.04)
  waiting for transfers between devices: 752 us -> 0 us
  blocking collectives: 287 us -> 0 us
  local copies, waits for them, and re-layouts: 74.5 us -> 4.93 us
  starting transfers between devices: 65.3 us -> 0 us
  Pallas kernels: 0 us -> 49.4 us
  other arithmetic: 47.1 us -> 0 us
  between operations: 20.2 us -> 0.73 us
    unnamed x7 -> x0, waiting for transfers between devices: 525 us -> none
    reduce_scatter x1 -> x0, waiting for transfers between devices: 210 us -> none  [per_device(): lax.psum_scatter(grad_five, 'view', scatter_dimension=1, tiled=True)]
    all_gather x5 -> x0, blocking collectives: 175 us -> none  [the longest x1 43.4 us: per_device(): lax.all_gather(centers, 'view', axis=1, tiled=True)]
    unnamed x1 -> x0, blocking collectives: 112 us -> none
    all_to_all x2 -> x0, starting transfers between devices: 65.1 us -> none  [the longest x1 61.7 us: per_device(): lax.all_to_all(picked, 'img', split_axis=1, concat_axis=1, tiled=True)]
    pallas_call x0 -> x1, Pallas kernels: none -> 49.4 us  [per_device(): pl.pallas_call(functools.partial(train_kernel, n_img, n_view, sizes), out...]
    unnamed x192 -> x28, local copies, waits for them, and re-layouts: 24.8 us -> 4.93 us
    scatter-add x2 -> x0, other arithmetic: 18.8 us -> none  [the longest x1 12.5 us: per_device(): shard_grad = jnp.zeros(proj_rows.shape, jnp.float32).at[:, send_slots.res...]
  transfers between devices with their start and end apart: 6 -> 0, of which waited for: 6 -> 0; matrix products, arithmetic and copies ran while one was open for 2% -> 0% of each run, Pallas kernels for 0% -> 0%
where the time goes in v1:
time: 55.3 us; the launch traced here: 55.1 us
  Pallas kernels  49.4 us (89%)
  local copies, waits for them, and re-layouts  4.93 us (9%)
  between operations  0.73 us (1%)
    pallas_call x1, Pallas kernels, per_device(): pl.pallas_call(functools.partial(train_kernel, n_img, n_view, sizes), out...  49.4 us
    unnamed x28, local copies, waits for them, and re-layouts  4.93 us

profile of v1, /device:TPU:1, one launch (start us, length us, event | category | flops | bytes accessed | tf_op | source)
XLA Modules:
  0.0 55.1 jit_solution(18204588064911915898)
XLA Ops:
  0.6 0.0 copy-start.9
  0.6 0.0 copy-start
  0.7 0.8 %copy.18.cameras_ref = f32[32,3]{1,0:T(8,128)S(1)} copy(f32[32,3]{0,1:T(4,128)} %param.16) | data formatting | bytes 768 | tf_op args[5]
  1.4 0.0 copy-done.9
  1.4 0.0 copy-start.3
  1.4 0.0 copy-start.4
  1.5 0.0 copy-start.5
  1.5 0.0 copy-start.6
  1.5 0.0 copy-start.7
  1.5 0.0 copy-start.8
  1.5 0.6 %copy-done.1 = s32[1,1,16,128]{3,2,1,0:T(8,128)S(1)} copy-done((s32[1,1,16,128]{3,2,1,0:T(8,128)S(1)}, s32[1,1,16,128]{3,2,1,0:T(8,128)}, u32[]{:S(2)}) %copy-start.1) | copy-done | bytes 8216
  2.1 0.0 copy-done.2
  2.1 0.0 copy-done.3
  2.1 0.0 copy-done.4
  2.2 0.0 copy-done.5
  2.2 0.0 copy-done.7
  2.2 0.0 copy-done.8
  2.2 49.4 %shard_map.154 = (f32[4,3,256]{2,1,0:T(4,128)S(1)}, f32[3,128]{1,0:T(4,128)S(1)}, f32[3,128]{1,0:T(4,128)S(1)}, f32[4,128]{1,0:T(4,128)S(1)}, f32[1,128]{1,0:T(1,128)S(1)}, /*index=5*/f32[48,128]{1,0:T(8,128)S(1)}) custom-call(f32[32,3]{1,0:T(8,128)S(1)} %copy.18.cameras_ref, f32[3,128]{1,0:T(4,128)S(1)} %copy-done.3, f32[3,128]{1,0:T(4,128)S(1)} %copy-done.4, ...), custom_call_target="tpu_custom_call" | custom-call | tf_op jit(solution)/shard_map/pallas_call | solution.py:589
  51.6 0.6 %copy.19 = f32[1,1,4,3,256]{4,2,3,1,0:T(4,128)} copy(f32[1,1,4,3,256]{4,3,2,1,0:T(4,128)S(1)} %bitcast.11) | data formatting | bytes 24576
  52.2 0.6 %copy.27 = f32[3,128]{1,0:T(4,128)} copy(f32[3,128]{1,0:T(4,128)S(1)} %get-tuple-element.31) | data formatting | bytes 3072
  52.8 0.6 %copy.28 = f32[3,128]{1,0:T(4,128)} copy(f32[3,128]{1,0:T(4,128)S(1)} %get-tuple-element.32) | data formatting | bytes 3072
  53.4 0.6 %copy.29 = f32[4,128]{1,0:T(4,128)} copy(f32[4,128]{1,0:T(4,128)S(1)} %get-tuple-element.33) | data formatting | bytes 4096
  54.0 0.5 copy.30
  54.5 0.6 %copy.31 = f32[48,128]{1,0:T(8,128)} copy(f32[48,128]{1,0:T(8,128)S(1)} %get-tuple-element.35) | data formatting | bytes 49152
  (5 shorter events, 0.0 us)
Async XLA Ops:
  0.6 0.8 %copy-start.9 = (f32[1,1,4,3,256]{4,2,3,1,0:T(4,128)S(1)}, f32[1,1,4,3,256]{4,2,3,1,0:T(4,128)}, u32[]{:S(2)}) copy-start(f32[1,1,4,3,256]{4,2,3,1,0:T(4,128)} %param.21) | copy-start | bytes 36868
  0.6 0.9 %copy-start = (f32[48,128]{1,0:T(8,128)S(1)}, f32[48,128]{1,0:T(8,128)}, u32[]{:S(2)}) copy-start(f32[48,128]{1,0:T(8,128)} %harm_ref.1) | copy-start | bytes 73732
  1.4 0.7 %copy-start.1 = (s32[1,1,16,128]{3,2,1,0:T(8,128)S(1)}, s32[1,1,16,128]{3,2,1,0:T(8,128)}, u32[]{:S(2)}) copy-start(s32[1,1,16,128]{3,2,1,0:T(8,128)} %param.20) | copy-start | bytes 24580
  1.4 0.7 %copy-start.2 = (s32[1,1,4,256]{3,2,1,0:T(4,128)S(1)}, s32[1,1,4,256]{3,2,1,0:T(4,128)}, u32[]{:S(2)}) copy-start(s32[1,1,4,256]{3,2,1,0:T(4,128)} %param.17) | copy-start | bytes 12292
  1.4 0.7 %copy-start.3 = (f32[3,128]{1,0:T(4,128)S(1)}, f32[3,128]{1,0:T(4,128)}, u32[]{:S(2)}) copy-start(f32[3,128]{1,0:T(4,128)} %centers_ref.1) | copy-start | bytes 4612
  1.4 0.7 %copy-start.4 = (f32[3,128]{1,0:T(4,128)S(1)}, f32[3,128]{1,0:T(4,128)}, u32[]{:S(2)}) copy-start(f32[3,128]{1,0:T(4,128)} %scales_ref.1) | copy-start | bytes 4612
  1.5 0.7 %copy-start.5 = (f32[4,128]{1,0:T(4,128)S(1)}, f32[4,128]{1,0:T(4,128)}, u32[]{:S(2)}) copy-start(f32[4,128]{1,0:T(4,128)} %quats_ref.1) | copy-start | bytes 6148
  1.5 0.7 %copy-start.6 = (f32[128]{0:T(128)S(1)}, f32[128]{0:T(128)}, u32[]{:S(2)}) copy-start(f32[128]{0:T(128)} %param.14) | copy-start | bytes 1540
  1.5 0.7 %copy-start.7 = (s32[1,1,4]{2,1,0:T(1,128)S(1)}, s32[1,1,4]{2,1,0:T(1,128)}, u32[]{:S(2)}) copy-start(s32[1,1,4]{2,1,0:T(1,128)} %param.18) | copy-start | bytes 52
  1.5 0.7 %copy-start.8 = (s32[1,1,4]{2,1,0:T(1,128)S(1)}, s32[1,1,4]{2,1,0:T(1,128)}, u32[]{:S(2)}) copy-start(s32[1,1,4]{2,1,0:T(1,128)} %param.19) | copy-start | bytes 52

commit v2 on v1

--- a/solution.py
+++ b/solution.py
@@ -11,6 +11,7 @@
 ROWS = 9
 LANES = 128
 PIX = 256
+MINOR = {"view": 4, "img": 2}
 FINE_ROWS = (2, 3, 4)
 LOG2E = 1.4426950408889634
 CAMERA_DISTANCE = 4.0
@@ -51,13 +52,10 @@
 
 
 def rotations(cameras, count):
-    cosines, sines = jnp.cos(cameras), jnp.sin(cameras)
-
-    def column(values, k):
-        return jnp.broadcast_to(values[:, k : k + 1], (count, LANES))
-
-    ca, cb, cg = (column(cosines, k) for k in range(3))
-    sa, sb, sg = (column(sines, k) for k in range(3))
+    turns = jnp.concatenate([jnp.cos(cameras), jnp.sin(cameras)], axis=0).T
+    ca, cb, cg, sa, sb, sg = (
+        jnp.broadcast_to(turns[:, k : k + 1], (count, LANES)) for k in range(6)
+    )
     return [
         [cg * ca, cg * sa * sb - sg * cb, cg * sa * cb + sg * sb],
         [sg * ca, sg * sa * sb + cg * cb, sg * sa * cb - cg * sb],
@@ -313,7 +311,32 @@
     return picture, grads
 
 
+def ring(size, steps):
+    return min(steps, size - steps)
+
+
+def farthest_first(axis, size):
+    minor = MINOR[axis]
+    major = size // minor
+    offsets = [(a, b) for a in range(major) for b in range(minor) if a or b]
+    return sorted(offsets, key=lambda o: -ring(major, o[0]) - ring(minor, o[1]) * (axis == "view"))
+
+
+def neighbour(me, offset, axis, size):
+    minor = MINOR[axis]
+    major = size // minor
+
+    def wrap(value, limit):
+        return jnp.where(value >= limit, value - limit, value)
+
+    return wrap(lax.div(me, minor) + offset[0], major) * minor + wrap(
+        lax.rem(me, minor) + offset[1], minor
+    )
+
+
 def exchange(axis, me, size, source, landing, send_sem, recv_sem):
+    peers = [neighbour(me, offset, axis, size) for offset in farthest_first(axis, size)]
+
     def copy(peer, slot):
         return pltpu.make_async_remote_copy(
             src_ref=source(peer),
@@ -324,59 +347,50 @@
             device_id_type=pl.DeviceIdType.MESH,
         )
 
-    def start(step, carry):
-        copy(lax.rem(me + step, size), me).start()
-        return carry
-
-    def sent(step, carry):
-        copy(lax.rem(me + step, size), me).wait_send()
-        return carry
-
-    lax.fori_loop(1, size, start, 0)
+    for peer in peers:
+        copy(peer, me).start()
 
     def arrived(peer):
         copy(peer, peer).wait_recv()
 
-    return arrived, lambda: lax.fori_loop(1, size, sent, 0)
+    def sent():
+        for peer in peers:
+            copy(peer, me).wait_send()
+
+    return peers[::-1], arrived, sent
 
 
 def greet(axis, me, size, barrier):
-    def signal(step, carry):
+    for offset in farthest_first(axis, size):
         pl.semaphore_signal(
             barrier,
             inc=1,
-            device_id={axis: lax.rem(me + step, size)},
+            device_id={axis: neighbour(me, offset, axis, size)},
             device_id_type=pl.DeviceIdType.MESH,
         )
-        return carry
-
-    lax.fori_loop(1, size, signal, 0)
-
-
-def picker(index, size):
-    blocks = index.shape[0]
-    high, low = lax.shift_right_logical(index, 7), lax.bitwise_and(index, 127)
-    highs = [jnp.broadcast_to(high[b : b + 1], (8, LANES)) for b in range(blocks)]
-    lows = [jnp.broadcast_to(low[b : b + 1], (8, LANES)) for b in range(blocks)]
-
-    def add(number, table, picks):
-        geometry, opacity = picks
-        front = table[0:8]
-        last = jnp.broadcast_to(table[8:9], (8, LANES))
-        geometry = tuple(
-            jnp.where(highs[b] == number, lane_pick(front, lows[b]), geometry[b])
-            for b in range(blocks)
-        )
-        opacity = tuple(
-            jnp.where(
-                high[8 * g : 8 * g + 8] == number, lane_pick(last, low[8 * g : 8 * g + 8]), opacity[g]
-            )
-            for g in range(blocks // 8)
-        )
-        return geometry, opacity
-
-    zero = jnp.zeros((8, LANES), F32)
-    return add, ((zero,) * blocks, (zero,) * (blocks // 8))
+
+
+def split_rows(block):
+    parts, lasts = [], []
+    front, last = block[0:8], block[8:9]
+    for _ in range(3):
+        parts.append(front.astype(BF16).astype(F32))
+        lasts.append(last.astype(BF16).astype(F32))
+        front, last = front - parts[-1], last - lasts[-1]
+    filler = jnp.zeros((5, LANES), F32)
+    return jnp.concatenate(parts + lasts + [filler], axis=0).astype(BF16)
+
+
+def pick(table_ref, high, hot):
+    groups = table_ref.shape[1]
+    table = jnp.concatenate(
+        [table_ref[half].reshape(32 * groups, LANES) for half in range(2)], axis=1
+    )
+    found = dot(table, hot)
+    total = sum(
+        jnp.where(high == g, found[32 * g : 32 * g + 32], 0.0) for g in range(groups)
+    )
+    return total[0:8] + total[8:16] + total[16:24], total[24:25] + total[25:26] + total[26:27]
 
 
 def scatter_sides(index, groups):
@@ -384,7 +398,7 @@
     high, low = lax.shift_right_logical(index, 8), lax.bitwise_and(index, 255)
     mask = lax.broadcasted_iota(jnp.int32, (groups, count), 0) == high
     hot = lax.broadcasted_iota(jnp.int32, (256, count), 0) == low
-    return mask, jnp.where(hot, 1.0, 0.0).astype(BF16)
+    return high, mask, jnp.where(hot, 1.0, 0.0).astype(BF16)
 
 
 def scatter(rows, mask, hot):
@@ -409,17 +423,17 @@
     n_img,
     n_view,
     sizes,
-    cameras_ref,
-    centers_ref,
-    scales_ref,
-    quats_ref,
-    logits_ref,
-    harm_ref,
-    lists_ref,
-    counts_ref,
-    ids_ref,
-    slots_ref,
-    grad_ref,
+    cameras_in,
+    centers_in,
+    scales_in,
+    quats_in,
+    logits_in,
+    harm_in,
+    slots_in,
+    lists_in,
+    counts_in,
+    ids_in,
+    grad_in,
     picture_ref,
     out_centers_ref,
     out_scales_ref,
@@ -434,14 +448,54 @@
     recv_three,
     send_four,
     recv_four,
+    cameras_ref,
+    centers_ref,
+    scales_ref,
+    quats_ref,
+    logits_ref,
+    harm_ref,
+    slots_ref,
+    lists_ref,
+    counts_ref,
+    ids_ref,
+    grad_ref,
+    view_table,
+    img_table,
+    slot_hot,
+    entry_hot,
     view_sems,
     img_sems,
+    load_sems,
 ):
     focal, half_w, half_h = sizes
     img, view = lax.axis_index("img"), lax.axis_index("view")
     barrier = pltpu.get_barrier_semaphore()
+    loads = [
+        pltpu.make_async_copy(source, target, load_sems.at[k])
+        for k, (source, target) in enumerate(
+            (
+                (cameras_in, cameras_ref),
+                (centers_in, centers_ref),
+                (scales_in, scales_ref),
+                (quats_in, quats_ref),
+                (logits_in, logits_ref),
+                (harm_in, harm_ref),
+                (slots_in, slots_ref),
+                (lists_in, lists_ref),
+                (counts_in, counts_ref),
+                (ids_in, ids_ref),
+                (grad_in, grad_ref),
+            )
+        )
+    ]
+    for load in loads[:6]:
+        load.start()
     greet("view", view, n_view, barrier)
     greet("img", img, n_img, barrier)
+    for load in loads[6:]:
+        load.start()
+    for load in loads[:6]:
+        load.wait()
 
     rot = rotations(cameras_ref[...], n_view)
     centers = [centers_ref[c : c + 1, :] for c in range(3)]
@@ -454,64 +508,63 @@
         send_one[:, r, :] = value
     send_one[:, 8, :] = jnp.broadcast_to(opacity, (n_view, LANES))
 
+    for load in loads[6:]:
+        load.wait()
     pl.semaphore_wait(barrier, n_view + n_img - 2)
-    arrived, sent_one = exchange(
+    peers, arrived, sent_one = exchange(
         "view", view, n_view, lambda p: send_one.at[p], recv_one, view_sems.at[0], view_sems.at[1]
     )
 
-    add, picks = picker(slots_ref[...], n_view)
-    picks = add(view, send_one[view], picks)
-
-    def take_view(step, picks):
-        peer = lax.rem(view + step, n_view)
-        arrived(peer)
-        return add(peer, recv_one[peer], picks)
-
-    geometry, last = lax.fori_loop(1, n_view, take_view, picks)
+    slot_index = jnp.concatenate([slots_ref[d : d + 1, :] for d in range(n_img)], axis=1)
+    slot_high, slot_mask, hot = scatter_sides(slot_index, n_view // 2)
+    slot_hot[...] = hot
+    view_table[lax.rem(view, 2), lax.div(view, 2)] = split_rows(send_one[view])
+    for at in range(0, n_view - 1, 8):
+        for peer in peers[at : at + 8]:
+            arrived(peer)
+        for peer in peers[at : at + 8]:
+            view_table[lax.rem(peer, 2), lax.div(peer, 2)] = split_rows(recv_one[peer])
+    geometry, last = pick(view_table, slot_high, slot_hot[...])
     for d in range(n_img):
-        send_two[d, 0:8, :] = geometry[d]
-        send_two[d, 8:9, :] = last[d // 8][d % 8 : d % 8 + 1]
-
-    arrived, sent_two = exchange(
+        send_two[d, 0:8, :] = geometry[:, LANES * d : LANES * d + LANES]
+        send_two[d, 8:9, :] = last[:, LANES * d : LANES * d + LANES]
+
+    peers, arrived, sent_two = exchange(
         "img", img, n_img, lambda p: send_two.at[p], recv_two, img_sems.at[0], img_sems.at[1]
     )
 
     tiles = lists_ref.shape[0]
     lists = lists_ref[...]
-    blocks = jnp.concatenate(
-        [lists[t : t + 1, LANES * h : LANES * h + LANES] for t in range(tiles) for h in range(2)], axis=0
-    )
     entry_index = jnp.concatenate([lists[t : t + 1] for t in range(tiles)], axis=1)
-    entry_mask, entry_hot = scatter_sides(entry_index, n_img // 2)
+    entry_high, entry_mask, hot = scatter_sides(entry_index, n_img // 2)
+    entry_hot[...] = hot
     before, after = triangle(False), triangle(True)
-    add, picks = picker(blocks, n_img)
-    picks = add(img, send_two[img], picks)
-
-    def take_img(step, picks):
-        peer = lax.rem(img + step, n_img)
-        arrived(peer)
-        return add(peer, recv_two[peer], picks)
-
-    geometry, last = lax.fori_loop(1, n_img, take_img, picks)
+    img_table[lax.rem(img, 2), lax.div(img, 2)] = split_rows(send_two[img])
+    for at in range(0, n_img - 1, 8):
+        for peer in peers[at : at + 8]:
+            arrived(peer)
+        for peer in peers[at : at + 8]:
+            img_table[lax.rem(peer, 2), lax.div(peer, 2)] = split_rows(recv_two[peer])
+    geometry, last = pick(img_table, entry_high, entry_hot[...])
     row_grads = [[] for _ in range(ROWS)]
     for t in range(tiles):
-        entries = jnp.concatenate([geometry[2 * t], geometry[2 * t + 1]], axis=1)
-        solid = jnp.concatenate([last[0][2 * t : 2 * t + 1], last[0][2 * t + 1 : 2 * t + 2]], axis=1)
-        grad = grad_ref[t]
+        entries = geometry[:, PIX * t : PIX * t + PIX]
+        solid = last[:, PIX * t : PIX * t + PIX]
+        grad = grad_ref[:, t, :]
         high = grad.astype(BF16).astype(F32)
         grad_t = jnp.concatenate([high, high, grad - high], axis=0).T.astype(BF16)
         picture, grads = render_tile(
             entries, solid, counts_ref[t], ids_ref[t], grad, grad_t, before, after
         )
-        picture_ref[t] = picture
+        picture_ref[:, t, :] = picture
         for r in range(ROWS):
             row_grads[r].append(grads[r])
 
     rows = [jnp.concatenate(parts, axis=1) for parts in row_grads]
-    for r, total in enumerate(scatter(rows, entry_mask, entry_hot)):
+    for r, total in enumerate(scatter(rows, entry_mask, entry_hot[...])):
         for h in range(2):
             send_three[:, h, r, :] = total[:, LANES * h : LANES * h + LANES]
-    arrived, sent_three = exchange(
+    peers, arrived, sent_three = exchange(
         "img",
         img,
         n_img,
@@ -521,22 +574,16 @@
         img_sems.at[3],
     )
     recv_three[img] = send_three[lax.div(img, 2), lax.rem(img, 2)]
-    slot_index = jnp.concatenate([slots_ref[d : d + 1, :] for d in range(n_img)], axis=1)
-    slot_mask, slot_hot = scatter_sides(slot_index, n_view // 2)
-
-    def take_back(step, carry):
-        arrived(lax.rem(img + step, n_img))
-        return carry
-
-    lax.fori_loop(1, n_img, take_back, 0)
+    for peer in peers:
+        arrived(peer)
 
     rows = [
         jnp.concatenate([recv_three[d, r : r + 1, :] for d in range(n_img)], axis=1) for r in range(ROWS)
     ]
-    for r, total in enumerate(scatter(rows, slot_mask, slot_hot)):
+    for r, total in enumerate(scatter(rows, slot_mask, slot_hot[...])):
         for h in range(2):
             send_four[:, h, r, :] = total[:, LANES * h : LANES * h + LANES]
-    arrived, sent_four = exchange(
+    peers, arrived, sent_four = exchange(
         "view",
         view,
         n_view,
@@ -547,11 +594,8 @@
     )
     recv_four[view] = send_four[lax.div(view, 2), lax.rem(view, 2)]
 
-    def take_home(step, carry):
-        arrived(lax.rem(view + step, n_view))
-        return carry
-
-    lax.fori_loop(1, n_view, take_home, 0)
+    for peer in peers:
+        arrived(peer)
 
     grads = [recv_four[:, r, :] for r in range(ROWS)]
     dcenters, dfactor = project_back(rot, factor, harm_ref, focal, saved, grads, out_harm_ref)
@@ -566,6 +610,18 @@
     sent_two()
     sent_three()
     sent_four()
+
+
+def place_kernel(*refs):
+    *arrays, sems = refs
+    count = len(arrays) // 2
+    moves = [
+        pltpu.make_async_copy(arrays[k], arrays[count + k], sems.at[k]) for k in range(count)
+    ]
+    for move in moves:
+        move.start()
+    for move in moves:
+        move.wait()
 
 
 def per_device(
@@ -584,20 +640,34 @@
     n_img, n_view = lax.axis_size("img"), lax.axis_size("view")
     tiles = tile_ids.shape[2]
     sizes = (16.0 * TW, 8.0 * TW, 8.0 * (n_img * tiles // TW))
-    vmem, smem = pl.BlockSpec(memory_space=pltpu.VMEM), pl.BlockSpec(memory_space=pltpu.SMEM)
+    vmem, hbm = pl.BlockSpec(memory_space=pltpu.VMEM), pl.BlockSpec(memory_space=pltpu.HBM)
     per_view, per_img = (n_view, ROWS, LANES), (n_img, ROWS, LANES)
-    out = pl.pallas_call(
+    inputs = (
+        cameras.T,
+        centers,
+        log_scales,
+        quaternions,
+        logits.reshape(1, -1),
+        harmonics,
+        send_index[0, 0],
+        tile_lists[0, 0],
+        tile_counts[0, 0],
+        tile_ids[0, 0],
+        pixel_grad[0, 0].transpose(1, 0, 2),
+    )
+    shapes = [
+        jax.ShapeDtypeStruct((3, tiles, PIX), F32),
+        jax.ShapeDtypeStruct((3, LANES), F32),
+        jax.ShapeDtypeStruct((3, LANES), F32),
+        jax.ShapeDtypeStruct((4, LANES), F32),
+        jax.ShapeDtypeStruct((1, LANES), F32),
+        jax.ShapeDtypeStruct((48, LANES), F32),
+    ]
+    results = pl.pallas_call(
         functools.partial(train_kernel, n_img, n_view, sizes),
-        out_shape=(
-            jax.ShapeDtypeStruct((tiles, 3, PIX), F32),
-            jax.ShapeDtypeStruct((3, LANES), F32),
-            jax.ShapeDtypeStruct((3, LANES), F32),
-            jax.ShapeDtypeStruct((4, LANES), F32),
-            jax.ShapeDtypeStruct((1, LANES), F32),
-            jax.ShapeDtypeStruct((48, LANES), F32),
-        ),
-        in_specs=[vmem] * 7 + [smem] * 2 + [vmem] * 2,
-        out_specs=(vmem,) * 6,
+        out_shape=shapes,
+        in_specs=[hbm] * len(inputs),
+        out_specs=[vmem] * len(shapes),
         scratch_shapes=[
             pltpu.VMEM(per_view, F32),
             pltpu.VMEM(per_view, F32),
@@ -607,26 +677,33 @@
             pltpu.VMEM(per_img, F32),
             pltpu.VMEM((n_view // 2, 2, ROWS, LANES), F32),
             pltpu.VMEM(per_view, F32),
+        ]
+        + [
+            (pltpu.SMEM if value.shape == (tiles,) else pltpu.VMEM)(value.shape, value.dtype)
+            for value in inputs
+        ]
+        + [
+            pltpu.VMEM((2, n_view // 2, 32, LANES), BF16),
+            pltpu.VMEM((2, n_img // 2, 32, LANES), BF16),
+            pltpu.VMEM((256, n_img * LANES), BF16),
+            pltpu.VMEM((256, tiles * PIX), BF16),
             pltpu.SemaphoreType.DMA((4, n_view)),
             pltpu.SemaphoreType.DMA((4, n_img)),
+            pltpu.SemaphoreType.DMA((len(inputs),)),
         ],
         compiler_params=pltpu.CompilerParams(
-            collective_id=0, has_side_effects=True, vmem_limit_bytes=40 * 1024 * 1024
+            collective_id=0, has_side_effects=True, vmem_limit_bytes=63 * 1024 * 1024
         ),
-    )(
-        cameras,
-        centers,
-        log_scales,
-        quaternions,
-        logits.reshape(1, -1),
-        harmonics,
-        tile_lists[0, 0],
-        tile_counts[0, 0],
-        tile_ids[0, 0],
-        send_index[0, 0],
-        pixel_grad[0, 0],
-    )
-    return (out[0][None, None], out[1], out[2], out[3], out[4].reshape(-1), out[5])
+    )(*inputs)
+    out = pl.pallas_call(
+        place_kernel,
+        out_shape=shapes,
+        in_specs=[vmem] * len(shapes),
+        out_specs=[hbm] * len(shapes),
+        scratch_shapes=[pltpu.SemaphoreType.DMA((len(shapes),))],
+    )(*results)
+    picture = out[0].transpose(1, 0, 2)[None, None]
+    return (picture, out[1], out[2], out[3], out[4].reshape(-1), out[5])
 
 
 def solution(mesh):

time: 55.3 us -> 48.2 us (0.87)
  local copies, waits for them, and re-layouts: 4.93 us -> 0 us
  Pallas kernels: 49.4 us -> 47.3 us
    unnamed x28 -> x0, local copies, waits for them, and re-layouts: 4.93 us -> none
    pallas_call x1, Pallas kernels: 49.4 us -> 45.8 us  [per_device(): pl.pallas_call(functools.partial(train_kernel, n_img, n_view, sizes), out...]
    pallas_call x0 -> x1, Pallas kernels: none -> 1.45 us  [per_device(): pl.pallas_call(place_kernel, out_shape=shapes, in_specs=[vmem] * len(shap...]
where the time goes in v2:
time: 48.2 us; the launch traced here: 47.9 us
  Pallas kernels  47.3 us (98%)
  between operations  0.64 us (1%)
    pallas_call x1, Pallas kernels, per_device(): pl.pallas_call(functools.partial(train_kernel, n_img, n_view, sizes), out...  45.8 us
    pallas_call x1, Pallas kernels, per_device(): pl.pallas_call(place_kernel, out_shape=shapes, in_specs=[vmem] * len(shap...  1.45 us

profile of v2, /device:TPU:1, one launch (start us, length us, event | category | flops | bytes accessed | tf_op | source)
XLA Modules:
  0.0 47.9 jit_solution(11510089248855538843)
XLA Ops:
  0.6 45.8 %shard_map.154 = (f32[3,4,256]{2,1,0:T(4,128)}, f32[3,128]{1,0:T(4,128)}, f32[3,128]{1,0:T(4,128)}, f32[4,128]{1,0:T(4,128)}, f32[1,128]{1,0:T(1,128)}, /*index=5*/f32[48,128]{1,0:T(8,128)}) custom-call(f32[3,32]{1,0:T(4,128)} %bitcast.16, f32[3,128]{1,0:T(4,128)} %centers_in.1, f32[3,128]{1,0:T(4,128)} %scales_in.1, f32[4,128]{1,0:T(4,128)} %quats_in.1, ...), custom_call_target="tpu_custom_call" | custom-call | tf_op jit(solution)/shard_map/pallas_call | solution.py:666
  46.5 1.5 %shard_map.155 = (f32[3,4,256]{2,1,0:T(4,128)}, f32[3,128]{1,0:T(4,128)}, f32[3,128]{1,0:T(4,128)}, f32[4,128]{1,0:T(4,128)}, f32[1,128]{1,0:T(1,128)}, /*index=5*/f32[48,128]{1,0:T(8,128)}) custom-call(f32[3,4,256]{2,1,0:T(4,128)} %get-tuple-element.18.refs_0_, f32[3,128]{1,0:T(4,128)} %get-tuple-element.19.refs_1_, f32[3,128]{1,0:T(4,128)} %get-tuple-element.20.refs_2_, ...), custom_call_target="tpu_custom_call" | custom-call | tf_op jit(solution)/shard_map/pallas_call | solution.py:698

commit v3 on v2

--- a/solution.py
+++ b/solution.py
@@ -12,6 +12,7 @@
 LANES = 128
 PIX = 256
 MINOR = {"view": 4, "img": 2}
+LINES = 16
 FINE_ROWS = (2, 3, 4)
 LOG2E = 1.4426950408889634
 CAMERA_DISTANCE = 4.0
@@ -236,79 +237,108 @@
     return jnp.where(row > col if later else row < col, 1.0, 0.0).astype(BF16)
 
 
-def render_tile(geometry, opacity, count, tile, grad, grad_t, before, after):
-    entry = lax.broadcasted_iota(jnp.int32, (1, PIX), 1)
-    live = jnp.where(entry < count, opacity, 0.0)
-    left = (16 * lax.rem(tile, TW) + 8).astype(F32)
-    top = (16 * lax.div(tile, TW) + 8).astype(F32)
-    u, v = geometry[0:1] - left, geometry[1:2] - top
-    ca, cb, cc = geometry[2:3], geometry[3:4], geometry[4:5]
-    colour = geometry[5:8]
-    local = lax.broadcasted_iota(jnp.int32, (16, PIX), 0).astype(F32) - 7.5
-    dx, dy = local - u, local - v
-    part_a = (-0.5 * LOG2E * ca) * dx * dx
-    part_b = (-LOG2E * cb) * dx
-    part_c = (-0.5 * LOG2E * cc) * dy * dy
-    c_hi, c_lo = split_two(colour)
-    mix = jnp.concatenate([c_hi, c_lo, c_hi], axis=0)
-    reach = dot(grad_t, mix)
-    moments = [None, None, None]
-    w_hi_all, w_lo_all = [], []
-    for at in range(0, 16, 4):
-        alphas, logs = [], []
-        for line in range(at, at + 4):
-            power = part_a + part_b * dy[line : line + 1] + part_c[line : line + 1]
-            alphas.append(live * jnp.exp2(power))
+class Tile:
+    def __init__(self, geometry, opacity, count, number, grad, grad_t):
+        entry = lax.broadcasted_iota(jnp.int32, (1, PIX), 1)
+        self.live = jnp.where(entry < count, opacity, 0.0)
+        self.opacity = opacity
+        left = (16 * lax.rem(number, TW) + 8).astype(F32)
+        top = (16 * lax.div(number, TW) + 8).astype(F32)
+        self.u, self.v = geometry[0:1] - left, geometry[1:2] - top
+        self.conic = geometry[2:3], geometry[3:4], geometry[4:5]
+        ca, cb, cc = self.conic
+        self.local = lax.broadcasted_iota(jnp.int32, (16, PIX), 0).astype(F32) - 7.5
+        dx, self.dy = self.local - self.u, self.local - self.v
+        self.part_a = (-0.5 * LOG2E * ca) * dx * dx
+        self.part_b = (-LOG2E * cb) * dx
+        self.part_c = (-0.5 * LOG2E * cc) * self.dy * self.dy
+        self.colour = split_two(geometry[5:8])
+        self.grad, self.grad_t = grad, grad_t
+        c_hi, c_lo = self.colour
+        self.mix = jnp.concatenate([c_hi, c_lo, c_hi], axis=0)
+        self.moments = [None, None, None]
+        self.weights = []
+
+    def shade(self, at, before):
+        alphas = []
+        for line in range(at, at + LINES):
+            power = self.part_a + self.part_b * self.dy[line : line + 1] + self.part_c[line : line + 1]
+            alphas.append(self.live * jnp.exp2(power))
         alpha = jnp.concatenate(alphas, axis=0)
-        left_over = 1.0 - alpha
-        log_left = jnp.log2(left_over)
+        log_left = jnp.log2(1.0 - alpha)
         log_hi, log_lo = split_two(log_left)
-        weight = alpha * jnp.exp2(dot(log_hi, before) + dot(log_lo, before))
-        gain = weight * reach[16 * at : 16 * at + 64]
+        reach = dot(self.grad_t[16 * at : 16 * (at + LINES)], self.mix)
+        return at, alpha, log_left, dot(log_hi, before) + dot(log_lo, before), reach
+
+    def weigh(self, shaded, after):
+        at, alpha, log_left, log_trans, reach = shaded
+        weight = alpha * jnp.exp2(log_trans)
+        gain = weight * reach
         g_hi, g_lo = split_two(gain)
-        behind = dot(g_hi, after) + dot(g_lo, after)
-        back = gain - behind * (alpha / left_over)
-        w_hi, w_lo = split_two(weight)
-        w_hi_all.append(w_hi)
-        w_lo_all.append(w_lo)
-        for k in range(4):
+        self.weights.append(split_two(weight))
+        return at, alpha, log_left, gain, dot(g_hi, after) + dot(g_lo, after)
+
+    def collect(self, weighed):
+        at, alpha, log_left, gain, behind = weighed
+        back = gain - behind * (alpha * jnp.exp2(-log_left))
+        for k in range(LINES):
             piece = back[16 * k : 16 * k + 16]
             level = at + k - 7.5
             terms = (piece, level * piece, (level * level) * piece)
             for m in range(3):
-                moments[m] = terms[m] if moments[m] is None else moments[m] + terms[m]
-    w_hi = jnp.concatenate(w_hi_all, axis=0)
-    w_lo = jnp.concatenate(w_lo_all, axis=0)
-    both = jnp.concatenate([c_hi, c_lo], axis=0)
-    first = dot_nt(both, w_hi)
-    picture = first[0:3] + first[3:6] + dot_nt(c_hi, w_lo)
-    pg_hi, pg_lo = split_two(grad)
-    both = jnp.concatenate([pg_hi, pg_lo], axis=0)
-    first = dot(both, w_hi)
-    dcolour = first[0:3] + first[3:6] + dot(pg_hi, w_lo)
-
-    def total(value):
-        return jnp.sum(value, axis=0, keepdims=True)
-
-    m0, my, myy = (total(m) for m in moments)
-    mx, mxy = total(local * moments[0]), total(local * moments[1])
-    mxx = total(local * local * moments[0])
-    qx, qy = mx - u * m0, my - v * m0
-    qxx = mxx - u * (mx + qx)
-    qyy = myy - v * (my + qy)
-    qxy = mxy - u * my - v * qx
-    grads = [
-        ca * qx + cb * qy,
-        cb * qx + cc * qy,
-        -0.5 * qxx,
-        -qxy,
-        -0.5 * qyy,
-        dcolour[0:1],
-        dcolour[1:2],
-        dcolour[2:3],
-        m0 / opacity,
-    ]
-    return picture, grads
+                self.moments[m] = terms[m] if self.moments[m] is None else self.moments[m] + terms[m]
+
+    def finish(self):
+        w_hi = jnp.concatenate([w[0] for w in self.weights], axis=0)
+        w_lo = jnp.concatenate([w[1] for w in self.weights], axis=0)
+        c_hi, c_lo = self.colour
+        first = dot_nt(jnp.concatenate([c_hi, c_lo], axis=0), w_hi)
+        picture = first[0:3] + first[3:6] + dot_nt(c_hi, w_lo)
+        g_hi, g_lo = split_two(self.grad)
+        first = dot(jnp.concatenate([g_hi, g_lo], axis=0), w_hi)
+        dcolour = first[0:3] + first[3:6] + dot(g_hi, w_lo)
+
+        def total(value):
+            return jnp.sum(value, axis=0, keepdims=True)
+
+        u, v, (ca, cb, cc), local = self.u, self.v, self.conic, self.local
+        m0, my, myy = (total(m) for m in self.moments)
+        mx, mxy = total(local * self.moments[0]), total(local * self.moments[1])
+        mxx = total(local * local * self.moments[0])
+        qx, qy = mx - u * m0, my - v * m0
+        qxx = mxx - u * (mx + qx)
+        qyy = myy - v * (my + qy)
+        qxy = mxy - u * my - v * qx
+        grads = [
+            ca * qx + cb * qy,
+            cb * qx + cc * qy,
+            -0.5 * qxx,
+            -qxy,
+            -0.5 * qyy,
+            dcolour[0:1],
+            dcolour[1:2],
+            dcolour[2:3],
+            m0 / self.opacity,
+        ]
+        return picture, grads
+
+
+def render(tiles, before, after):
+    parts = [(tile, at) for tile in tiles for at in range(0, 16, LINES)]
+    shaded, weighed, done = [], [], []
+    for step in range(len(parts) + 2):
+        if step >= 2:
+            tile, at = parts[step - 2]
+            tile.collect(weighed[step - 2])
+            weighed[step - 2] = None
+            if at + LINES == 16:
+                done.append(tile.finish())
+        if 1 <= step <= len(parts):
+            weighed.append(parts[step - 1][0].weigh(shaded[step - 1], after))
+            shaded[step - 1] = None
+        if step < len(parts):
+            shaded.append(parts[step][0].shade(parts[step][1], before))
+    return done
 
 
 def ring(size, steps):
@@ -381,15 +411,33 @@
     return jnp.concatenate(parts + lasts + [filler], axis=0).astype(BF16)
 
 
-def pick(table_ref, high, hot):
-    groups = table_ref.shape[1]
-    table = jnp.concatenate(
-        [table_ref[half].reshape(32 * groups, LANES) for half in range(2)], axis=1
-    )
-    found = dot(table, hot)
-    total = sum(
-        jnp.where(high == g, found[32 * g : 32 * g + 32], 0.0) for g in range(groups)
-    )
+def by_distance(axis, size, cuts):
+    major = size // MINOR[axis]
+    return [
+        [a for a in range(major) if low < ring(major, a) <= high]
+        for low, high in zip((-1, *cuts), (*cuts, major))
+    ]
+
+
+def pick(axis, me, size, cuts, arrived, landing, high, hot):
+    minor = MINOR[axis]
+    total = None
+    for group in by_distance(axis, size, cuts):
+        numbers = []
+        for a in group:
+            for b in range(minor):
+                if a or b:
+                    arrived(neighbour(me, (a, b), axis, size))
+            first = lax.div(neighbour(me, (a, 0), axis, size), minor) * (minor // 2)
+            numbers += [first + k for k in range(minor // 2)]
+        table = [
+            jnp.concatenate([split_rows(landing[2 * n]), split_rows(landing[2 * n + 1])], axis=1)
+            for n in numbers
+        ]
+        found = dot(jnp.concatenate(table, axis=0), hot)
+        for k, n in enumerate(numbers):
+            part = jnp.where(high == n, found[32 * k : 32 * k + 32], 0.0)
+            total = part if total is None else total + part
     return total[0:8] + total[8:16] + total[16:24], total[24:25] + total[25:26] + total[26:27]
 
 
@@ -402,21 +450,31 @@
 
 
 def scatter(rows, mask, hot):
-    groups = mask.shape[0]
-    sides, owners = [], []
+    return scattered(scatter_parts(rows, mask, hot), mask.shape[0], len(rows))
+
+
+def scatter_parts(rows, mask, hot):
+    sides = []
     for r, row in enumerate(rows):
-        for _ in range(3 if r in FINE_ROWS else 2):
+        for _ in range(parts_of(r)):
             high = row.astype(BF16).astype(F32)
             sides.append(jnp.where(mask, high, 0.0))
-            owners.append(r)
             row = row - high
-    if len(sides) * groups % 16:
+    if len(sides) * mask.shape[0] % 16:
         sides.append(jnp.zeros_like(sides[0]))
-    out = dot_nt(jnp.concatenate(sides, axis=0).astype(BF16), hot)
-    return [
-        sum(out[groups * k : groups * (k + 1)] for k, owner in enumerate(owners) if owner == r)
-        for r in range(len(rows))
-    ]
+    return dot_nt(jnp.concatenate(sides, axis=0).astype(BF16), hot)
+
+
+def parts_of(row):
+    return 3 if row in FINE_ROWS else 2
+
+
+def scattered(out, groups, count):
+    sums, at = [], 0
+    for r in range(count):
+        sums.append(sum(out[groups * k : groups * (k + 1)] for k in range(at, at + parts_of(r))))
+        at += parts_of(r)
+    return sums
 
 
 def train_kernel(
@@ -459,8 +517,6 @@
     counts_ref,
     ids_ref,
     grad_ref,
-    view_table,
-    img_table,
     slot_hot,
     entry_hot,
     view_sems,
@@ -516,15 +572,11 @@
     )
 
     slot_index = jnp.concatenate([slots_ref[d : d + 1, :] for d in range(n_img)], axis=1)
-    slot_high, slot_mask, hot = scatter_sides(slot_index, n_view // 2)
-    slot_hot[...] = hot
-    view_table[lax.rem(view, 2), lax.div(view, 2)] = split_rows(send_one[view])
-    for at in range(0, n_view - 1, 8):
-        for peer in peers[at : at + 8]:
-            arrived(peer)
-        for peer in peers[at : at + 8]:
-            view_table[lax.rem(peer, 2), lax.div(peer, 2)] = split_rows(recv_one[peer])
-    geometry, last = pick(view_table, slot_high, slot_hot[...])
+    slot_high, _, hot = scatter_sides(slot_index, n_view // 2)
+    for d in range(n_img):
+        slot_hot[d] = hot[:, LANES * d : LANES * d + LANES]
+    recv_one[view] = send_one[view]
+    geometry, last = pick("view", view, n_view, (1, 3), arrived, recv_one, slot_high, hot)
     for d in range(n_img):
         send_two[d, 0:8, :] = geometry[:, LANES * d : LANES * d + LANES]
         send_two[d, 8:9, :] = last[:, LANES * d : LANES * d + LANES]
@@ -539,28 +591,20 @@
     entry_high, entry_mask, hot = scatter_sides(entry_index, n_img // 2)
     entry_hot[...] = hot
     before, after = triangle(False), triangle(True)
-    img_table[lax.rem(img, 2), lax.div(img, 2)] = split_rows(send_two[img])
-    for at in range(0, n_img - 1, 8):
-        for peer in peers[at : at + 8]:
-            arrived(peer)
-        for peer in peers[at : at + 8]:
-            img_table[lax.rem(peer, 2), lax.div(peer, 2)] = split_rows(recv_two[peer])
-    geometry, last = pick(img_table, entry_high, entry_hot[...])
-    row_grads = [[] for _ in range(ROWS)]
+    recv_two[img] = send_two[img]
+    geometry, last = pick("img", img, n_img, (3,), arrived, recv_two, entry_high, hot)
+    work = []
     for t in range(tiles):
-        entries = geometry[:, PIX * t : PIX * t + PIX]
-        solid = last[:, PIX * t : PIX * t + PIX]
         grad = grad_ref[:, t, :]
         high = grad.astype(BF16).astype(F32)
         grad_t = jnp.concatenate([high, high, grad - high], axis=0).T.astype(BF16)
-        picture, grads = render_tile(
-            entries, solid, counts_ref[t], ids_ref[t], grad, grad_t, before, after
-        )
-        picture_ref[:, t, :] = picture
-        for r in range(ROWS):
-            row_grads[r].append(grads[r])
-
-    rows = [jnp.concatenate(parts, axis=1) for parts in row_grads]
+        at = slice(PIX * t, PIX * t + PIX)
+        work.append(Tile(geometry[:, at], last[:, at], counts_ref[t], ids_ref[t], grad, grad_t))
+    rendered = render(work, before, after)
+    for t in range(tiles):
+        picture_ref[:, t, :] = rendered[t][0]
+
+    rows = [jnp.concatenate([grads[r] for _, grads in rendered], axis=1) for r in range(ROWS)]
     for r, total in enumerate(scatter(rows, entry_mask, entry_hot[...])):
         for h in range(2):
             send_three[:, h, r, :] = total[:, LANES * h : LANES * h + LANES]
@@ -574,13 +618,24 @@
         img_sems.at[3],
     )
     recv_three[img] = send_three[lax.div(img, 2), lax.rem(img, 2)]
-    for peer in peers:
-        arrived(peer)
-
-    rows = [
-        jnp.concatenate([recv_three[d, r : r + 1, :] for d in range(n_img)], axis=1) for r in range(ROWS)
-    ]
-    for r, total in enumerate(scatter(rows, slot_mask, slot_hot[...])):
+    out = None
+    for group in by_distance("img", n_img, (1, 3)):
+        places = []
+        for a in group:
+            for b in range(MINOR["img"]):
+                places.append(neighbour(img, (a, b), "img", n_img))
+                if a or b:
+                    arrived(places[-1])
+        rows = [
+            jnp.concatenate([recv_three[p, r : r + 1, :] for p in places], axis=1) for r in range(ROWS)
+        ]
+        high = lax.shift_right_logical(
+            jnp.concatenate([slots_ref[pl.ds(p, 1), :] for p in places], axis=1), 8
+        )
+        mask = lax.broadcasted_iota(jnp.int32, (n_view // 2, high.shape[1]), 0) == high
+        part = scatter_parts(rows, mask, jnp.concatenate([slot_hot[p] for p in places], axis=1))
+        out = part if out is None else out + part
+    for r, total in enumerate(scattered(out, n_view // 2, ROWS)):
         for h in range(2):
             send_four[:, h, r, :] = total[:, LANES * h : LANES * h + LANES]
     peers, arrived, sent_four = exchange(
@@ -665,7 +720,7 @@
     ]
     results = pl.pallas_call(
         functools.partial(train_kernel, n_img, n_view, sizes),
-        out_shape=shapes,
+        out_shape=[pltpu.VMEM(shape.shape, shape.dtype) for shape in shapes],
         in_specs=[hbm] * len(inputs),
         out_specs=[vmem] * len(shapes),
         scratch_shapes=[
@@ -683,9 +738,7 @@
             for value in inputs
         ]
         + [
-            pltpu.VMEM((2, n_view // 2, 32, LANES), BF16),
-            pltpu.VMEM((2, n_img // 2, 32, LANES), BF16),
-            pltpu.VMEM((256, n_img * LANES), BF16),
+            pltpu.VMEM((n_img, 256, LANES), BF16),
             pltpu.VMEM((256, tiles * PIX), BF16),
             pltpu.SemaphoreType.DMA((4, n_view)),
             pltpu.SemaphoreType.DMA((4, n_img)),
@@ -701,7 +754,7 @@
         in_specs=[vmem] * len(shapes),
         out_specs=[hbm] * len(shapes),
         scratch_shapes=[pltpu.SemaphoreType.DMA((len(shapes),))],
-    )(*results)
+    )(*(pltpu.with_memory_space_constraint(value, pltpu.VMEM) for value in results))
     picture = out[0].transpose(1, 0, 2)[None, None]
     return (picture, out[1], out[2], out[3], out[4].reshape(-1), out[5])
 

time: 48.2 us -> 45.4 us (0.942)
  Pallas kernels: 47.3 us -> 44.5 us
    pallas_call x1, Pallas kernels: 45.8 us -> 43.8 us  [per_device(): pl.pallas_call(functools.partial(train_kernel, n_img, n_view, sizes), out...]
    pallas_call x1, Pallas kernels: 1.45 us -> 0.68 us  [per_device(): pl.pallas_call(place_kernel, out_shape=shapes, in_specs=[vmem] * len(shap...]
where the time goes in v3:
time: 45.4 us; the launch traced here: 45.2 us
  Pallas kernels  44.5 us (98%)
  between operations  0.64 us (1%)
    pallas_call x1, Pallas kernels, per_device(): pl.pallas_call(functools.partial(train_kernel, n_img, n_view, sizes), out...  43.8 us

profile of v3, /device:TPU:1, one launch (start us, length us, event | category | flops | bytes accessed | tf_op | source)
XLA Modules:
  0.0 45.2 jit_solution(5466876452710644146)
XLA Ops:
  0.6 43.8 %shard_map.154 = (f32[3,4,256]{2,1,0:T(4,128)S(1)}, f32[3,128]{1,0:T(4,128)S(1)}, f32[3,128]{1,0:T(4,128)S(1)}, f32[4,128]{1,0:T(4,128)S(1)}, f32[1,128]{1,0:T(1,128)S(1)}, /*index=5*/f32[48,128]{1,0:T(8,128)S(1)}) custom-call(f32[3,32]{1,0:T(4,128)} %bitcast.16, f32[3,128]{1,0:T(4,128)} %centers_in.1, f32[3,128]{1,0:T(4,128)} %scales_in.1, ...), custom_call_target="tpu_custom_call" | custom-call | tf_op jit(solution)/shard_map/pallas_call | solution.py:721
  44.5 0.7 %shard_map.155 = (f32[3,4,256]{2,1,0:T(4,128)}, f32[3,128]{1,0:T(4,128)}, f32[3,128]{1,0:T(4,128)}, f32[4,128]{1,0:T(4,128)}, f32[1,128]{1,0:T(1,128)}, /*index=5*/f32[48,128]{1,0:T(8,128)}) custom-call(f32[3,4,256]{2,1,0:T(4,128)S(1)} %get-tuple-element.18.refs_0_, f32[3,128]{1,0:T(4,128)S(1)} %get-tuple-element.19.refs_1_, ...), custom_call_target="tpu_custom_call" | custom-call | tf_op jit(solution)/shard_map/pallas_call | solution.py:751

commit v4 on v3

--- a/solution.py
+++ b/solution.py
@@ -294,7 +294,7 @@
         c_hi, c_lo = self.colour
         first = dot_nt(jnp.concatenate([c_hi, c_lo], axis=0), w_hi)
         picture = first[0:3] + first[3:6] + dot_nt(c_hi, w_lo)
-        g_hi, g_lo = split_two(self.grad)
+        g_hi, g_lo = self.grad
         first = dot(jnp.concatenate([g_hi, g_lo], axis=0), w_hi)
         dcolour = first[0:3] + first[3:6] + dot(g_hi, w_lo)
 
@@ -591,15 +591,18 @@
     entry_high, entry_mask, hot = scatter_sides(entry_index, n_img // 2)
     entry_hot[...] = hot
     before, after = triangle(False), triangle(True)
+    pixels = []
+    for t in range(tiles):
+        grad = grad_ref[:, t, :]
+        high = grad.astype(BF16).astype(F32)
+        columns = jnp.concatenate([high, high, grad - high], axis=0).T.astype(BF16)
+        pixels.append((split_two(grad), columns))
     recv_two[img] = send_two[img]
     geometry, last = pick("img", img, n_img, (3,), arrived, recv_two, entry_high, hot)
     work = []
     for t in range(tiles):
-        grad = grad_ref[:, t, :]
-        high = grad.astype(BF16).astype(F32)
-        grad_t = jnp.concatenate([high, high, grad - high], axis=0).T.astype(BF16)
         at = slice(PIX * t, PIX * t + PIX)
-        work.append(Tile(geometry[:, at], last[:, at], counts_ref[t], ids_ref[t], grad, grad_t))
+        work.append(Tile(geometry[:, at], last[:, at], counts_ref[t], ids_ref[t], *pixels[t]))
     rendered = render(work, before, after)
     for t in range(tiles):
         picture_ref[:, t, :] = rendered[t][0]
@@ -648,6 +651,10 @@
         view_sems.at[3],
     )
     recv_four[view] = send_four[lax.div(view, 2), lax.rem(view, 2)]
+    sent_one()
+    sent_two()
+    sent_three()
+    sent_four()
 
     for peer in peers:
         arrived(peer)
@@ -661,10 +668,6 @@
     for k in range(4):
         out_quats_ref[k : k + 1, :] = dquat[k]
     out_logits_ref[...] = over_cameras(grads[8]) * opacity * (1.0 - opacity)
-    sent_one()
-    sent_two()
-    sent_three()
-    sent_four()
 
 
 def place_kernel(*refs):

time: 45.4 us -> 45.2 us (level)
  no operation moved by 1% of the time
where the time goes in v4:
time: 45.2 us; the launch traced here: 45 us
  Pallas kernels  44.4 us (98%)
  between operations  0.64 us (1%)
    pallas_call x1, Pallas kernels, per_device(): pl.pallas_call(functools.partial(train_kernel, n_img, n_view, sizes), out...  43.7 us

profile of v4, /device:TPU:1, one launch (start us, length us, event | category | flops | bytes accessed | tf_op | source)
XLA Modules:
  0.0 45.0 jit_solution(15997740266830895437)
XLA Ops:
  0.6 43.7 %shard_map.154 = (f32[3,4,256]{2,1,0:T(4,128)S(1)}, f32[3,128]{1,0:T(4,128)S(1)}, f32[3,128]{1,0:T(4,128)S(1)}, f32[4,128]{1,0:T(4,128)S(1)}, f32[1,128]{1,0:T(1,128)S(1)}, /*index=5*/f32[48,128]{1,0:T(8,128)S(1)}) custom-call(f32[3,32]{1,0:T(4,128)} %bitcast.16, f32[3,128]{1,0:T(4,128)} %centers_in.1, f32[3,128]{1,0:T(4,128)} %scales_in.1, ...), custom_call_target="tpu_custom_call" | custom-call | tf_op jit(solution)/shard_map/pallas_call | solution.py:724
  44.3 0.7 %shard_map.155 = (f32[3,4,256]{2,1,0:T(4,128)}, f32[3,128]{1,0:T(4,128)}, f32[3,128]{1,0:T(4,128)}, f32[4,128]{1,0:T(4,128)}, f32[1,128]{1,0:T(1,128)}, /*index=5*/f32[48,128]{1,0:T(8,128)}) custom-call(f32[3,4,256]{2,1,0:T(4,128)S(1)} %get-tuple-element.18.refs_0_, f32[3,128]{1,0:T(4,128)S(1)} %get-tuple-element.19.refs_1_, ...), custom_call_target="tpu_custom_call" | custom-call | tf_op jit(solution)/shard_map/pallas_call | solution.py:754

commit v5 on v4

--- a/solution.py
+++ b/solution.py
@@ -288,12 +288,16 @@
             for m in range(3):
                 self.moments[m] = terms[m] if self.moments[m] is None else self.moments[m] + terms[m]
 
+    def picture(self):
+        c_hi, c_lo = self.colour
+        w_hi, w_lo = self.weights
+        first = dot_nt(jnp.concatenate([c_hi, c_lo], axis=0), w_hi)
+        return first[0:3] + first[3:6] + dot_nt(c_hi, w_lo)
+
     def finish(self):
         w_hi = jnp.concatenate([w[0] for w in self.weights], axis=0)
         w_lo = jnp.concatenate([w[1] for w in self.weights], axis=0)
-        c_hi, c_lo = self.colour
-        first = dot_nt(jnp.concatenate([c_hi, c_lo], axis=0), w_hi)
-        picture = first[0:3] + first[3:6] + dot_nt(c_hi, w_lo)
+        self.weights = w_hi, w_lo
         g_hi, g_lo = self.grad
         first = dot(jnp.concatenate([g_hi, g_lo], axis=0), w_hi)
         dcolour = first[0:3] + first[3:6] + dot(g_hi, w_lo)
@@ -320,7 +324,7 @@
             dcolour[2:3],
             m0 / self.opacity,
         ]
-        return picture, grads
+        return grads
 
 
 def render(tiles, before, after):
@@ -365,7 +369,12 @@
 
 
 def exchange(axis, me, size, source, landing, send_sem, recv_sem):
-    peers = [neighbour(me, offset, axis, size) for offset in farthest_first(axis, size)]
+    def peers(places=None):
+        return [
+            neighbour(me, offset, axis, size)
+            for offset in farthest_first(axis, size)
+            if places is None or offset[0] in places
+        ]
 
     def copy(peer, slot):
         return pltpu.make_async_remote_copy(
@@ -377,17 +386,18 @@
             device_id_type=pl.DeviceIdType.MESH,
         )
 
-    for peer in peers:
-        copy(peer, me).start()
+    def start(places=None):
+        for peer in peers(places):
+            copy(peer, me).start()
 
     def arrived(peer):
         copy(peer, peer).wait_recv()
 
     def sent():
-        for peer in peers:
+        for peer in peers():
             copy(peer, me).wait_send()
 
-    return peers[::-1], arrived, sent
+    return start, arrived, sent
 
 
 def greet(axis, me, size, barrier):
@@ -567,9 +577,10 @@
     for load in loads[6:]:
         load.wait()
     pl.semaphore_wait(barrier, n_view + n_img - 2)
-    peers, arrived, sent_one = exchange(
+    start, arrived, sent_one = exchange(
         "view", view, n_view, lambda p: send_one.at[p], recv_one, view_sems.at[0], view_sems.at[1]
     )
+    start()
 
     slot_index = jnp.concatenate([slots_ref[d : d + 1, :] for d in range(n_img)], axis=1)
     slot_high, _, hot = scatter_sides(slot_index, n_view // 2)
@@ -581,9 +592,10 @@
         send_two[d, 0:8, :] = geometry[:, LANES * d : LANES * d + LANES]
         send_two[d, 8:9, :] = last[:, LANES * d : LANES * d + LANES]
 
-    peers, arrived, sent_two = exchange(
+    start, arrived, sent_two = exchange(
         "img", img, n_img, lambda p: send_two.at[p], recv_two, img_sems.at[0], img_sems.at[1]
     )
+    start()
 
     tiles = lists_ref.shape[0]
     lists = lists_ref[...]
@@ -604,14 +616,11 @@
         at = slice(PIX * t, PIX * t + PIX)
         work.append(Tile(geometry[:, at], last[:, at], counts_ref[t], ids_ref[t], *pixels[t]))
     rendered = render(work, before, after)
-    for t in range(tiles):
-        picture_ref[:, t, :] = rendered[t][0]
-
-    rows = [jnp.concatenate([grads[r] for _, grads in rendered], axis=1) for r in range(ROWS)]
+    rows = [jnp.concatenate([grads[r] for grads in rendered], axis=1) for r in range(ROWS)]
     for r, total in enumerate(scatter(rows, entry_mask, entry_hot[...])):
         for h in range(2):
             send_three[:, h, r, :] = total[:, LANES * h : LANES * h + LANES]
-    peers, arrived, sent_three = exchange(
+    start, arrived, sent_three = exchange(
         "img",
         img,
         n_img,
@@ -620,28 +629,11 @@
         img_sems.at[2],
         img_sems.at[3],
     )
+    start()
     recv_three[img] = send_three[lax.div(img, 2), lax.rem(img, 2)]
-    out = None
-    for group in by_distance("img", n_img, (1, 3)):
-        places = []
-        for a in group:
-            for b in range(MINOR["img"]):
-                places.append(neighbour(img, (a, b), "img", n_img))
-                if a or b:
-                    arrived(places[-1])
-        rows = [
-            jnp.concatenate([recv_three[p, r : r + 1, :] for p in places], axis=1) for r in range(ROWS)
-        ]
-        high = lax.shift_right_logical(
-            jnp.concatenate([slots_ref[pl.ds(p, 1), :] for p in places], axis=1), 8
-        )
-        mask = lax.broadcasted_iota(jnp.int32, (n_view // 2, high.shape[1]), 0) == high
-        part = scatter_parts(rows, mask, jnp.concatenate([slot_hot[p] for p in places], axis=1))
-        out = part if out is None else out + part
-    for r, total in enumerate(scattered(out, n_view // 2, ROWS)):
-        for h in range(2):
-            send_four[:, h, r, :] = total[:, LANES * h : LANES * h + LANES]
-    peers, arrived, sent_four = exchange(
+    for t in range(tiles):
+        picture_ref[:, t, :] = work[t].picture()
+    start, arrived_home, sent_four = exchange(
         "view",
         view,
         n_view,
@@ -650,14 +642,55 @@
         view_sems.at[2],
         view_sems.at[3],
     )
+    minor = MINOR["view"]
+    major, pairs = n_view // minor, minor // 2
+    places = sorted(range(major), key=lambda a: -ring(major, a))
+    numbers = []
+    for a in places:
+        first = lax.div(neighbour(view, (a, 0), "view", n_view), minor) * pairs
+        numbers += [first + k for k in range(pairs)]
+    row = lax.broadcasted_iota(jnp.int32, (len(numbers), 1), 0)
+    order = sum(jnp.where(row == k, n, 0) for k, n in enumerate(numbers))
+    half = len(numbers) // 2
+    sums = []
+    groups = by_distance("img", n_img, (1, 3))
+    for group in groups:
+        blocks = []
+        for a in group:
+            for b in range(MINOR["img"]):
+                blocks.append(neighbour(img, (a, b), "img", n_img))
+                if a or b:
+                    arrived(blocks[-1])
+        rows = [
+            jnp.concatenate([recv_three[p, r : r + 1, :] for p in blocks], axis=1) for r in range(ROWS)
+        ]
+        high = lax.shift_right_logical(
+            jnp.concatenate([slots_ref[pl.ds(p, 1), :] for p in blocks], axis=1), 8
+        )
+        hot = jnp.concatenate([slot_hot[p] for p in blocks], axis=1)
+        for h in range(2):
+            mask = order[half * h : half * h + half] == high
+            part = scatter_parts(rows, mask, hot)
+            if group is groups[0]:
+                sums.append(part)
+            else:
+                sums[h] = sums[h] + part
+            if group is groups[-1]:
+                for r, total in enumerate(scattered(sums[h], half, ROWS)):
+                    for k in range(half):
+                        for side in range(2):
+                            send_four[numbers[half * h + k], side, r : r + 1, :] = total[
+                                k : k + 1, LANES * side : LANES * side + LANES
+                            ]
+                start(places[major // 2 * h : major // 2 * (h + 1)])
     recv_four[view] = send_four[lax.div(view, 2), lax.rem(view, 2)]
     sent_one()
     sent_two()
     sent_three()
     sent_four()
 
-    for peer in peers:
-        arrived(peer)
+    for offset in farthest_first("view", n_view)[::-1]:
+        arrived_home(neighbour(view, offset, "view", n_view))
 
     grads = [recv_four[:, r, :] for r in range(ROWS)]
     dcenters, dfactor = project_back(rot, factor, harm_ref, focal, saved, grads, out_harm_ref)

time: 45.2 us -> 44.8 us (level)
  no operation moved by 1% of the time
where the time goes in v5:
time: 44.8 us; the launch traced here: 44.6 us
  Pallas kernels  44 us (98%)
  between operations  0.64 us (1%)
    pallas_call x1, Pallas kernels, per_device(): pl.pallas_call(functools.partial(train_kernel, n_img, n_view, sizes), out...  43.3 us

profile of v5, /device:TPU:1, one launch (start us, length us, event | category | flops | bytes accessed | tf_op | source)
XLA Modules:
  0.0 44.6 jit_solution(15667405143909289675)
XLA Ops:
  0.6 43.3 %shard_map.154 = (f32[3,4,256]{2,1,0:T(4,128)S(1)}, f32[3,128]{1,0:T(4,128)S(1)}, f32[3,128]{1,0:T(4,128)S(1)}, f32[4,128]{1,0:T(4,128)S(1)}, f32[1,128]{1,0:T(1,128)S(1)}, /*index=5*/f32[48,128]{1,0:T(8,128)S(1)}) custom-call(f32[3,32]{1,0:T(4,128)} %bitcast.16, f32[3,128]{1,0:T(4,128)} %centers_in.1, f32[3,128]{1,0:T(4,128)} %scales_in.1, ...), custom_call_target="tpu_custom_call" | custom-call | tf_op jit(solution)/shard_map/pallas_call | solution.py:757
  44.0 0.7 %shard_map.155 = (f32[3,4,256]{2,1,0:T(4,128)}, f32[3,128]{1,0:T(4,128)}, f32[3,128]{1,0:T(4,128)}, f32[4,128]{1,0:T(4,128)}, f32[1,128]{1,0:T(1,128)}, /*index=5*/f32[48,128]{1,0:T(8,128)}) custom-call(f32[3,4,256]{2,1,0:T(4,128)S(1)} %get-tuple-element.18.refs_0_, f32[3,128]{1,0:T(4,128)S(1)} %get-tuple-element.19.refs_1_, ...), custom_call_target="tpu_custom_call" | custom-call | tf_op jit(solution)/shard_map/pallas_call | solution.py:787
